TPU v7x, 512 devices: a whole 4x4x16 slice. The times are simulated.
512 devices in a mesh: replica: 32 (over z, y_lo), fsdp: 16 (over x, y_hi, core).
Axes of the slice: x: 4, y: 4 (y_hi: 2, y_lo: 2; y = y_hi * 2 + y_lo), z: 16, core: 2. Of those that a mesh axis runs over, the one named last changes fastest.
Arguments:
- tokens: bfloat16 [98304, 8192], P(('replica', 'fsdp')), may hold values from -6 to 6
- master: float32 [8192, 512], P(('fsdp', 'replica')), may hold values from -1 to 1, as said below
- momentum: float32 [8192, 512], P(('fsdp', 'replica')), may hold values from -0.046875 to 0.046875
- trained: bfloat16 [32, 8192, 512], P('replica', 'fsdp'), may hold values from -1 to 1, as said below
Outputs:
- new_master: float32 [8192, 512], P(('fsdp', 'replica'))
- new_momentum: float32 [8192, 512], P(('fsdp', 'replica'))
- refreshed: bfloat16 [8192, 512], P('fsdp')
- keys: float32 [98304, 512], P(('replica', 'fsdp'))
Inputs may be any that keep to these rules, and one draw needn't show every extreme that they name: master is a weight matrix of scale about 8192 ** -0.5. Each replica's trained weights are the bfloat16 start weights plus that replica's drift.
All inputs are finite; a program needn't handle non-finite values.
Results may differ from a plain program's by a relative error of at most 0.012.
Values may be sent and summed in bfloat16 or wider, within the bound.
No kernel may reach another device: no remote copies, remote signals or barrier semaphores. Data moves between devices by JAX's collectives and lax.ppermute only.
A program may use at most 64 MiB of HBM per device.

v0:
```python
import jax
import jax.numpy as jnp
from jax import lax
from jax.sharding import PartitionSpec as P

outer_rate = 0.7
decay_factor = 0.9


def outer_step(summed, master_rows, momentum_rows, replicas):
    rounded = lax.optimization_barrier(master_rows.astype(jnp.bfloat16))
    begin_weights = rounded.astype(jnp.float32)
    pseudo = begin_weights - summed / replicas
    new_momentum = decay_factor * momentum_rows + pseudo
    new_master = master_rows - outer_rate * (pseudo + decay_factor * new_momentum)
    return (new_master, new_momentum)


def local(tokens, master, momentum, trained):
    replicas = lax.axis_size("replica")
    local_shard = trained[0].astype(jnp.float32)
    summed = lax.psum_scatter(local_shard, "replica", scatter_dimension=0, tiled=True)
    new_master, new_momentum = outer_step(summed, master, momentum, replicas)
    refreshed = lax.all_gather(new_master.astype(jnp.bfloat16), "replica", axis=0, tiled=True)
    key_values = jnp.dot(
        tokens,
        lax.all_gather(refreshed, "fsdp", axis=0, tiled=True),
        preferred_element_type=jnp.float32,
    )
    return (new_master, new_momentum, refreshed, key_values)


def solution(mesh):
    in_specs = (
        P(("replica", "fsdp"), None),
        P(("fsdp", "replica"), None),
        P(("fsdp", "replica"), None),
        P("replica", "fsdp", None),
    )
    out_specs = (
        P(("fsdp", "replica"), None),
        P(("fsdp", "replica"), None),
        P("fsdp", None),
        P(("replica", "fsdp"), None),
    )
    return jax.shard_map(local, mesh=mesh, in_specs=in_specs, out_specs=out_specs, check_vma=False)
```

profile of v0, /device:TPU:1, one launch (start us, length us, event | category | flops | bytes accessed | tf_op | source)
XLA Modules:
  0.0 322.8 jit_solution(16526535200551391562)
XLA Ops:
  7.2 0.0 copy-start
  7.2 0.0 reduce-scatter.2.cloned.1.call-start
  7.2 2.3 bitcast_convert_fusion
  9.5 0.0 reduce-scatter.2.cloned.1.call-update
  9.5 0.0 all-gather.2.cloned.1.call-start
  9.6 0.8 convert_element_type.15
  10.4 118.0 %reduce-scatter.2.cloned.1.call-done = f32[16,512]{1,0:T(8,128)} async-done(((f32[512,512]{1,0:T(8,128)}), f32[16,512]{1,0:T(8,128)}) %reduce-scatter.2.cloned.1.call-update) | async-done | bytes 32784 | tf_op jit(solution)/shard_map/reduce_scatter | solution.py:22
  128.3 1.4 fusion
  129.8 53.2 %all_gather.6 = bf16[512,512]{1,0:T(8,128)(2,1)} all-gather(bf16[16,512]{1,0:T(8,128)(2,1)S(1)} %get-tuple-element.4), channel_id=1, replica_groups=mesh['replica'=32,'fsdp'=16] {'replica'}, dimensions={0}, use_global_device_ids=true | all-gather | bytes 540672 | tf_op jit(solution)/shard_map/all_gather | solution.py:24
  182.9 0.0 all-gather.2.cloned.1.call-update
  183.0 126.2 %all-gather.2.cloned.1.call-done = bf16[8192,512]{1,0:T(8,128)(2,1)} async-done(((bf16[512,512]{1,0:T(8,128)(2,1)}), bf16[8192,512]{1,0:T(8,128)(2,1)}) %all-gather.2.cloned.1.call-update) | async-done | bytes 8388624 | tf_op jit(solution)/shard_map/all_gather | solution.py:27
  309.2 0.0 copy-done
  309.2 0.0 copy-start.1
  309.2 6.0 %convolution_bitcast_fusion = f32[192,512]{1,0:T(8,128)} fusion(bf16[192,8192]{1,0:T(8,128)(2,1)S(1)} %copy-done, bf16[8192,512]{1,0:T(8,128)(2,1)} %all-gather.2.cloned.1.call-done), kind=kOutput, calls=%fused_computation | convolution fusion | flops 1610612736 | bytes 11927552 | tf_op jit(solution)/shard_map/dot_general | solution.py:25
  315.1 0.0 copy-done.1
  315.1 0.8 copy.9
Async XLA Ops:
  7.2 302.0 %copy-start = (bf16[192,8192]{1,0:T(8,128)(2,1)S(1)}, bf16[192,8192]{1,0:T(8,128)(2,1)}, u32[]{:S(2)}) copy-start(bf16[192,8192]{1,0:T(8,128)(2,1)} %param.4) | copy-start | bytes 9437188
  7.2 121.2 %reduce-scatter.2.cloned.1.call-start = ((), (), s32[]{:S(2)}) async-start(), calls=%async_computation.1 | async-start | bytes 1081344 | tf_op jit(solution)/shard_map/reduce_scatter | solution.py:22
  9.5 299.6 %all-gather.2.cloned.1.call-start = ((), (), s32[]{:S(2)}) async-start(), calls=%async_computation.2 | async-start | bytes 8912896 | tf_op jit(solution)/shard_map/all_gather | solution.py:27
  309.2 6.0 %copy-start.1 = (bf16[512,512]{1,0:T(8,128)(2,1)S(1)}, bf16[512,512]{1,0:T(8,128)(2,1)}, u32[]{:S(2)}) copy-start(bf16[512,512]{1,0:T(8,128)(2,1)} %all_gather.6) | copy-start | bytes 1572868
Sparse Core Ops, SparseCore 0:
  10.8 117.4 reduce-scatter.1
  183.1 126.0 all-gather.1
where the time goes:
time: 323 us
  waiting for transfers between devices  244 us (76%)
  blocking collectives  53.2 us (16%)
  between operations  14 us (4%)
  matrix products  5.97 us (2%)
  other arithmetic  4.49 us (1%)
    all_gather x1, waiting for transfers between devices, local(): lax.all_gather(refreshed, 'fsdp', axis=0, tiled=True)  126 us
    reduce_scatter x1, waiting for transfers between devices, local(): lax.psum_scatter(local_shard, 'replica', scatter_dimension=0, tiled=True)  118 us
    all_gather x1, blocking collectives, local(): lax.all_gather(new_master.astype(jnp.bfloat16), 'replica', axis=0, tiled=...  53.2 us
  transfers between devices with their start and end apart: 2, of which 2 were waited for; matrix products, arithmetic and copies ran while one was open for 0% of the time, Pallas kernels for 0%

commit v1 on v0

v1 whole, which is shorter than its diff:
```python
import jax
import jax.numpy as jnp
from jax import lax
from jax.experimental import pallas as pl
from jax.experimental.pallas import tpu as pltpu
from jax.sharding import Mesh, PartitionSpec as P

outer_rate = 0.7
decay_factor = 0.9


def outer_step(summed, master_rows, momentum_rows, replicas):
    rounded = lax.optimization_barrier(master_rows.astype(jnp.bfloat16))
    begin_weights = rounded.astype(jnp.float32)
    pseudo = begin_weights - summed / replicas
    new_momentum = decay_factor * momentum_rows + pseudo
    new_master = master_rows - outer_rate * (pseudo + decay_factor * new_momentum)
    return (new_master, new_momentum)


def spread(block, axis, n):
    copies = jnp.broadcast_to(block[None], (n,) + block.shape)
    return lax.all_to_all(copies, axis, 0, 0, tiled=True)


def keys_kernel(at, own, other, t0, t1, t2, t3, out, fresh, w, t, o, sem_w, sem_t, sem_o, sem_f):
    x, yh, c = at[0], at[1], at[2]
    nl, nh = own.shape[:2]
    nx = t.shape[0]
    loads = []
    for h in range(nh):
        for l in range(nl):
            for i, (source, core) in enumerate(((own, c), (other, 1 - c))):
                copy = pltpu.make_async_copy(source.at[l, h], w.at[h, core, :, l], sem_w.at[i, h * nl + l])
                copy.start()
                loads.append(copy)
    taken = []
    for d, source in enumerate((t0, t1, t2, t3)):
        copy = pltpu.make_async_copy(source, t.at[d], sem_t.at[d])
        copy.start()
        taken.append(copy)
    for copy in loads:
        copy.wait()
    for l in range(nl):
        pltpu.make_async_copy(w.at[yh, c, :, l], fresh.at[:, l], sem_f.at[l]).start()
    weights = w[...].reshape(t.shape[2], out.shape[2])
    sent = []
    for d in range(nx):
        taken[d].wait()
        o[d] = jnp.dot(t[d], weights, preferred_element_type=jnp.float32).astype(o.dtype)
        copy = pltpu.make_async_copy(o.at[d], out.at[lax.rem(x + nx - d, nx)], sem_o.at[d])
        copy.start()
        sent.append(copy)
    for l in range(nl):
        pltpu.make_async_copy(w.at[yh, c, :, l], fresh.at[:, l], sem_f.at[l]).wait()
    for copy in sent:
        copy.wait()


def multiply(at, own, other, pieces):
    nl, nh, nz, rows, kv = own.shape
    nx = len(pieces)
    tok, part = pieces[0].shape
    hbm = pl.BlockSpec(memory_space=pl.ANY)
    return pl.pallas_call(
        keys_kernel,
        out_shape=(
            jax.ShapeDtypeStruct((nx, tok, kv), jnp.bfloat16),
            jax.ShapeDtypeStruct((nz, nl, rows, kv), jnp.bfloat16),
        ),
        in_specs=[pl.BlockSpec(memory_space=pltpu.SMEM)] + [hbm] * (2 + nx),
        out_specs=(hbm, hbm),
        scratch_shapes=[
            pltpu.VMEM((nh, 2, nz, nl, rows, kv), jnp.bfloat16),
            pltpu.VMEM((nx, tok, part), jnp.bfloat16),
            pltpu.VMEM((nx, tok, kv), jnp.bfloat16),
            pltpu.SemaphoreType.DMA((2, nh * nl)),
            pltpu.SemaphoreType.DMA((nx,)),
            pltpu.SemaphoreType.DMA((nx,)),
            pltpu.SemaphoreType.DMA((nl,)),
        ],
        compiler_params=pltpu.CompilerParams(vmem_limit_bytes=12 * 2**20),
        cost_estimate=pl.CostEstimate(
            flops=2 * nx * tok * part * kv, bytes_accessed=8 * 2**20, transcendentals=0
        ),
    )(at, own, other, *(pltpu.with_memory_space_constraint(p, pltpu.HBM) for p in pieces))


def local(tokens, master, momentum, trained):
    nz, nl, nx, nh, nc = (lax.axis_size(a) for a in ("z", "yl", "x", "yh", "c"))
    rows, kv = master.shape
    tok, depth = tokens.shape
    x, yh, c = lax.axis_index("x"), lax.axis_index("yh"), lax.axis_index("c")
    part = depth // nx

    owned = lax.all_to_all(trained[0].reshape(nz * nl, rows, kv), ("z", "yl"), 0, 0, tiled=True)
    summed = jnp.sum(owned.astype(jnp.float32), axis=0)
    new_master, new_momentum = outer_step(summed, master, momentum, nz * nl)
    fresh = new_master.astype(jnp.bfloat16)

    pieces = []
    for d in range(nx):
        piece = lax.dynamic_slice(tokens, (0, (x + d) % nx * part), (tok, part))
        if d:
            piece = lax.ppermute(piece, "x", [(i, (i + d) % nx) for i in range(nx)])
        pieces.append(piece)
    fresh, pieces[1], pieces[3] = lax.optimization_barrier((fresh, pieces[1], pieces[3]))

    rows_z = spread(fresh, "z", nz)
    rows_z, *pieces = lax.optimization_barrier((rows_z, *pieces))
    rows_y = spread(rows_z, ("yl", "yh"), nl * nh).reshape(nl, nh, nz, rows, kv)
    others = lax.ppermute(rows_y, "c", [(0, 1), (1, 0)])

    share, refreshed = multiply(jnp.stack([x, yh, c]).astype(jnp.int32), rows_y, others, pieces)
    share = lax.all_to_all(share, "x", 0, 0, tiled=True)
    key_values = jnp.sum(share.astype(jnp.float32), axis=0)
    return (new_master, new_momentum, refreshed.reshape(-1, kv), key_values)


def solution(mesh):
    fine = Mesh(mesh.devices.reshape(16, 2, 4, 2, 2), ("z", "yl", "x", "yh", "c"))
    replica, fsdp = ("z", "yl"), ("x", "yh", "c")
    in_specs = (
        P(replica + fsdp, None),
        P(fsdp + replica, None),
        P(fsdp + replica, None),
        P(replica, fsdp, None),
    )
    out_specs = (
        P(fsdp + replica, None),
        P(fsdp + replica, None),
        P(fsdp, None),
        P(replica + fsdp, None),
    )
    return jax.shard_map(local, mesh=fine, in_specs=in_specs, out_specs=out_specs, check_vma=False)
```

time: 323 us -> 123 us (0.38)
  waiting for transfers between devices: 244 us -> 41.5 us
  starting transfers between devices: 0.08 us -> 39.9 us
  blocking collectives: 53.2 us -> 29 us
  between operations: 14 us -> 0.8 us
  matrix products: 5.97 us -> 0 us
  Pallas kernels: 0 us -> 5.49 us
    all_gather x1 -> x0, waiting for transfers between devices: 126 us -> none  [local(): lax.all_gather(refreshed, 'fsdp', axis=0, tiled=True)]
    reduce_scatter x1 -> x0, waiting for transfers between devices: 118 us -> none  [local(): lax.psum_scatter(local_shard, 'replica', scatter_dimension=0, tiled=True)]
    all_gather x1 -> x0, blocking collectives: 53.2 us -> none  [local(): lax.all_gather(new_master.astype(jnp.bfloat16), 'replica', axis=0, tiled=...]
    all_to_all x0 -> x2, blocking collectives: none -> 29 us  [the longest x1 14.5 us: spread(): return lax.all_to_all(copies, axis, 0, 0, tiled=True)]
    all_to_all x0 -> x2, starting transfers between devices: none -> 24.9 us  [the longest x1 17.1 us: local(): lax.all_to_all(trained[0].reshape(nz * nl, rows, kv), ('z', 'yl'), 0, 0,...]
    all_to_all x0 -> x2, waiting for transfers between devices: none -> 21.5 us  [the longest x1 21.5 us: local(): lax.all_to_all(trained[0].reshape(nz * nl, rows, kv), ('z', 'yl'), 0, 0,...]
    ppermute x0 -> x4, waiting for transfers between devices: none -> 20 us  [the longest x3 17.8 us: local(): piece = lax.ppermute(piece, 'x', [(i, (i + d) % nx) for i in range(nx)])]
    ppermute x0 -> x4, starting transfers between devices: none -> 15 us  [the longest x3 8.22 us: local(): piece = lax.ppermute(piece, 'x', [(i, (i + d) % nx) for i in range(nx)])]
  transfers between devices with their start and end apart: 2 -> 6, of which waited for: 2 -> 3; matrix products, arithmetic and copies ran while one was open for 0% -> 3% of each run, Pallas kernels for 0% -> 0%
where the time goes in v1:
time: 123 us; the launch traced here: 122 us
  waiting for transfers between devices  41.5 us (34%)
  starting transfers between devices  39.9 us (32%)
  blocking collectives  29 us (24%)
  Pallas kernels  5.49 us (4%)
  local copies, waits for them, and re-layouts  3.9 us (3%)
  other arithmetic  1.66 us (1%)
    all_to_all x1, waiting for transfers between devices, local(): lax.all_to_all(trained[0].reshape(nz * nl, rows, kv), ('z', 'yl'), 0, 0,...  21.5 us
    ppermute x3, waiting for transfers between devices, local(): piece = lax.ppermute(piece, 'x', [(i, (i + d) % nx) for i in range(nx)])  17.8 us
    all_to_all x1, starting transfers between devices, local(): lax.all_to_all(trained[0].reshape(nz * nl, rows, kv), ('z', 'yl'), 0, 0,...  17.1 us
    all_to_all x1, blocking collectives, spread(): return lax.all_to_all(copies, axis, 0, 0, tiled=True)  14.5 us
    all_to_all x1, blocking collectives, local(): share = lax.all_to_all(share, 'x', 0, 0, tiled=True)  14.4 us
    ppermute x3, starting transfers between devices, local(): piece = lax.ppermute(piece, 'x', [(i, (i + d) % nx) for i in range(nx)])  8.22 us
    all_to_all x1, starting transfers between devices, spread(): return lax.all_to_all(copies, axis, 0, 0, tiled=True)  7.86 us
    ppermute x1, starting transfers between devices, local(): others = lax.ppermute(rows_y, 'c', [(0, 1), (1, 0)])  6.81 us
  transfers between devices with their start and end apart: 6, of which 3 were waited for; matrix products, arithmetic and copies ran while one was open for 3% of the time, Pallas kernels for 0%

profile of v1, /device:TPU:1, one launch (start us, length us, event | category | flops | bytes accessed | tf_op | source)
XLA Modules:
  0.0 122.2 jit_solution(12961435800227467604)
XLA Ops:
  0.6 17.1 %all-to-all-start = ((bf16[32,16,512]{2,1,0:T(8,128)(2,1)}), bf16[32,16,512]{2,1,0:T(8,128)(2,1)S(1)}, u32[]{:S(2)}, u32[]{:S(2)}) async-start(bf16[32,16,512]{2,1,0:T(8,128)(2,1)} %bitcast.8), calls=%async_computation | async-start | bytes 1048576 | tf_op jit(solution)/shard_map/all_to_all | solution.py:96
  17.7 0.0 copy-start
  17.8 0.0 copy-start.1
  17.8 3.0 %constant_dynamic-slice_fusion = (bf16[192,2048]{1,0:T(8,128)(2,1)S(1)}, bf16[192,2048]{1,0:T(8,128)(2,1)S(1)}, bf16[192,2048]{1,0:T(8,128)(2,1)S(1)}, bf16[192,2048]{1,0:T(8,128)(2,1)}) fusion(bf16[192,8192]{1,0:T(8,128)(2,1)} %param.4, s32[]{:T(128)S(6)} %select_n.38, s32[]{:T(128)S(6)} %select_n.34, s32[]{:T(128)S(6)} %select_n.32, s32[]{:T(128)S(6)} %select_n.36), kind=kLoop, calls=%fused_computation.5 | loop fusion | bytes 6291472 | tf_op jit(solution)/shard_map/dynamic_slice | solution.py:103
  20.8 4.4 %collective-permute-start.1 = (bf16[192,2048]{1,0:T(8,128)(2,1)S(1)}, bf16[192,2048]{1,0:T(8,128)(2,1)}, u32[]{:S(2)}, u32[]{:S(2)}) collective-permute-start(bf16[192,2048]{1,0:T(8,128)(2,1)S(1)} %get-tuple-element.28), channel_id=1, source_target_pairs={{0,12},{4,0},{8,4},{12,8},{1,13},{5,1},{9,5},{13,9},{2,14},{6,2},{... | collective-permute-start | bytes 2359304 | tf_op jit(solution)/shard_map/ppermute | solution.py:105
  25.2 1.9 %collective-permute-start = (bf16[192,2048]{1,0:T(8,128)(2,1)S(1)}, bf16[192,2048]{1,0:T(8,128)(2,1)}, u32[]{:S(2)}, u32[]{:S(2)}) collective-permute-start(bf16[192,2048]{1,0:T(8,128)(2,1)S(1)} %get-tuple-element.29), channel_id=1, source_target_pairs={{0,4},{4,8},{8,12},{12,0},{1,5},{5,9},{9,13},{13,1},{2,6},{6,10},{... | collective-permute-start | bytes 2359304 | tf_op jit(solution)/shard_map/ppermute | solution.py:105
  27.1 0.0 copy-done
  27.2 21.5 %all-to-all-done = bf16[32,16,512]{2,1,0:T(8,128)(2,1)S(1)} async-done(((bf16[32,16,512]{2,1,0:T(8,128)(2,1)}), bf16[32,16,512]{2,1,0:T(8,128)(2,1)S(1)}, u32[]{:S(2)}, u32[]{:S(2)}) %all-to-all-start) | async-done | bytes 524320 | tf_op jit(solution)/shard_map/all_to_all | solution.py:96
  48.7 0.1 convert_reduce_fusion.1
  48.7 0.0 copy-done.1
  48.8 0.6 fusion
  49.4 0.0 collective-permute-done.1.t3
  49.4 0.0 collective-permute-done.t1
  49.4 0.7 broadcast_in_dim.4
  50.1 7.9 %all-to-all-start.1 = ((bf16[16,16,512]{2,1,0:T(8,128)(2,1)}), bf16[16,16,512]{2,1,0:T(8,128)(2,1)S(1)}, u32[]{:S(2)}, u32[]{:S(2)}) async-start(bf16[16,16,512]{2,1,0:T(8,128)(2,1)} %broadcast_in_dim.4), calls=%async_computation.1 | async-start | bytes 524288 | tf_op jit(solution)/shard_map/all_to_all | solution.py:23
  58.0 1.9 %collective-permute-start.2 = (bf16[192,2048]{1,0:T(8,128)(2,1)S(1)}, bf16[192,2048]{1,0:T(8,128)(2,1)S(1)}, u32[]{:S(2)}, u32[]{:S(2)}) collective-permute-start(bf16[192,2048]{1,0:T(8,128)(2,1)S(1)} %get-tuple-element.27), channel_id=1, source_target_pairs={{0,8},{4,12},{8,0},{12,4},{1,9},{5,13},{9,1},{13,5},{2,10},{6,14},... | collective-permute-start | bytes 2359304 | tf_op jit(solution)/shard_map/ppermute | solution.py:105
  59.9 17.8 %collective-permute-done.2.t2 = bf16[192,2048]{1,0:T(8,128)(2,1)S(1)} collective-permute-done((bf16[192,2048]{1,0:T(8,128)(2,1)S(1)}, bf16[192,2048]{1,0:T(8,128)(2,1)S(1)}, u32[]{:S(2)}, u32[]{:S(2)}) %collective-permute-start.2) | collective-permute-done | bytes 786464 | tf_op jit(solution)/shard_map/ppermute | solution.py:105
  77.7 0.0 copy-start.2
  77.7 0.0 all-to-all-done.1
  77.7 0.1 broadcast_in_dim.5
  77.8 14.5 %all_to_all.20 = bf16[4,16,16,512]{3,2,1,0:T(8,128)(2,1)S(1)} all-to-all(bf16[4,16,16,512]{3,2,1,0:T(8,128)(2,1)S(1)} %broadcast_in_dim.5), channel_id=1, replica_groups=mesh['z'=16,'yl'=2,'x'=4,'yh'=2,'c'=2] {'yl','yh'}, dimensions={0} | all-to-all | bytes 2097152 | tf_op jit(solution)/shard_map/all_to_all | solution.py:23
  92.4 6.8 %collective-permute-start.3 = (bf16[2,2,16,16,512]{4,3,2,1,0:T(8,128)(2,1)S(1)}, bf16[2,2,16,16,512]{4,3,2,1,0:T(8,128)(2,1)S(1)}, u32[]{:S(2)}, u32[]{:S(2)}) collective-permute-start(bf16[2,2,16,16,512]{4,3,2,1,0:T(8,128)(2,1)S(1)} %bitcast.6), channel_id=1, source_target_pairs={{0,1},{1,0},{2,3},{3,2},{4,5},{5,4},{6,7},{7,6},{8,9},{9,8},{10,11... | collective-permute-start | bytes 3145736 | tf_op jit(solution)/shard_map/ppermute | solution.py:112
  99.2 0.1 pad_add_fusion.at
  99.3 2.2 %collective-permute-done.3.other = bf16[2,2,16,16,512]{4,3,2,1,0:T(8,128)(2,1)S(1)} collective-permute-done((bf16[2,2,16,16,512]{4,3,2,1,0:T(8,128)(2,1)S(1)}, bf16[2,2,16,16,512]{4,3,2,1,0:T(8,128)(2,1)S(1)}, u32[]{:S(2)}, u32[]{:S(2)}) %collective-permute-start.3) | collective-permute-done | bytes 1048608 | tf_op jit(solution)/shard_map/ppermute | solution.py:112
  101.5 0.0 copy-done.2
  101.5 5.5 %shard_map.75 = (bf16[4,192,512]{2,1,0:T(8,128)(2,1)S(1)}, bf16[16,2,16,512]{3,2,1,0:T(8,128)(2,1)}) custom-call(s32[3]{0:T(128)S(1)} %pad_add_fusion.at, bf16[2,2,16,16,512]{4,3,2,1,0:T(8,128)(2,1)S(1)} %bitcast.7, bf16[2,2,16,16,512]{4,3,2,1,0:T(8,128)(2,1)S(1)} %collective-permute-done.3.other, bf16[192,2048]{1,0:T(8,128)(2,1)} %get-tuple-element.18.t0, ...), custom_call_target="tpu_custom_call" | custom-call | flops 1610612736 | bytes 8388608 | tf_op jit(solution)/shard_map/pallas_call | solution.py:65
  107.0 14.4 %all_to_all.21 = bf16[4,192,512]{2,1,0:T(8,128)(2,1)S(1)} all-to-all(bf16[4,192,512]{2,1,0:T(8,128)(2,1)S(1)} %get-tuple-element.23), channel_id=1, replica_groups=mesh['z'=16,'yl'=2,'x'=4,'yh'=2,'c'=2] {'x'}, dimensions={0} | all-to-all | bytes 1572864 | tf_op jit(solution)/shard_map/all_to_all | solution.py:115
  121.4 0.9 convert_reduce_fusion
  (1 shorter events, 0.0 us)
Async XLA Ops:
  0.6 48.0 %all-to-all-start = ((bf16[32,16,512]{2,1,0:T(8,128)(2,1)}), bf16[32,16,512]{2,1,0:T(8,128)(2,1)S(1)}, u32[]{:S(2)}, u32[]{:S(2)}) async-start(bf16[32,16,512]{2,1,0:T(8,128)(2,1)} %bitcast.8), calls=%async_computation | async-start | bytes 1048576 | tf_op jit(solution)/shard_map/all_to_all | solution.py:96
  17.7 9.4 %copy-start = (f32[16,512]{1,0:T(8,128)S(1)}, f32[16,512]{1,0:T(8,128)}, u32[]{:S(2)}) copy-start(f32[16,512]{1,0:T(8,128)} %param.5) | copy-start | bytes 98308
  17.8 31.0 %copy-start.1 = (f32[16,512]{1,0:T(8,128)S(1)}, f32[16,512]{1,0:T(8,128)}, u32[]{:S(2)}) copy-start(f32[16,512]{1,0:T(8,128)} %param.6) | copy-start | bytes 98308
  20.8 28.6 %collective-permute-start.1 = (bf16[192,2048]{1,0:T(8,128)(2,1)S(1)}, bf16[192,2048]{1,0:T(8,128)(2,1)}, u32[]{:S(2)}, u32[]{:S(2)}) collective-permute-start(bf16[192,2048]{1,0:T(8,128)(2,1)S(1)} %get-tuple-element.28), channel_id=1, source_target_pairs={{0,12},{4,0},{8,4},{12,8},{1,13},{5,1},{9,5},{13,9},{2,14},{6,2},{... | collective-permute-start | bytes 2359304 | tf_op jit(solution)/shard_map/ppermute | solution.py:105
  25.2 24.2 %collective-permute-start = (bf16[192,2048]{1,0:T(8,128)(2,1)S(1)}, bf16[192,2048]{1,0:T(8,128)(2,1)}, u32[]{:S(2)}, u32[]{:S(2)}) collective-permute-start(bf16[192,2048]{1,0:T(8,128)(2,1)S(1)} %get-tuple-element.29), channel_id=1, source_target_pairs={{0,4},{4,8},{8,12},{12,0},{1,5},{5,9},{9,13},{13,1},{2,6},{6,10},{... | collective-permute-start | bytes 2359304 | tf_op jit(solution)/shard_map/ppermute | solution.py:105
  50.1 27.6 %all-to-all-start.1 = ((bf16[16,16,512]{2,1,0:T(8,128)(2,1)}), bf16[16,16,512]{2,1,0:T(8,128)(2,1)S(1)}, u32[]{:S(2)}, u32[]{:S(2)}) async-start(bf16[16,16,512]{2,1,0:T(8,128)(2,1)} %broadcast_in_dim.4), calls=%async_computation.1 | async-start | bytes 524288 | tf_op jit(solution)/shard_map/all_to_all | solution.py:23
  58.0 19.7 %collective-permute-start.2 = (bf16[192,2048]{1,0:T(8,128)(2,1)S(1)}, bf16[192,2048]{1,0:T(8,128)(2,1)S(1)}, u32[]{:S(2)}, u32[]{:S(2)}) collective-permute-start(bf16[192,2048]{1,0:T(8,128)(2,1)S(1)} %get-tuple-element.27), channel_id=1, source_target_pairs={{0,8},{4,12},{8,0},{12,4},{1,9},{5,13},{9,1},{13,5},{2,10},{6,14},... | collective-permute-start | bytes 2359304 | tf_op jit(solution)/shard_map/ppermute | solution.py:105
  77.7 23.8 %copy-start.2 = (bf16[192,2048]{1,0:T(8,128)(2,1)}, bf16[192,2048]{1,0:T(8,128)(2,1)S(1)}, u32[]{:S(2)}) copy-start(bf16[192,2048]{1,0:T(8,128)(2,1)S(1)} %collective-permute-done.2.t2) | copy-start | bytes 2359300
  92.4 9.1 %collective-permute-start.3 = (bf16[2,2,16,16,512]{4,3,2,1,0:T(8,128)(2,1)S(1)}, bf16[2,2,16,16,512]{4,3,2,1,0:T(8,128)(2,1)S(1)}, u32[]{:S(2)}, u32[]{:S(2)}) collective-permute-start(bf16[2,2,16,16,512]{4,3,2,1,0:T(8,128)(2,1)S(1)} %bitcast.6), channel_id=1, source_target_pairs={{0,1},{1,0},{2,3},{3,2},{4,5},{5,4},{6,7},{7,6},{8,9},{9,8},{10,11... | collective-permute-start | bytes 3145736 | tf_op jit(solution)/shard_map/ppermute | solution.py:112

commit v2 on v0

v2 whole, which is shorter than its diff:
```python
import itertools
import math

import jax
import jax.numpy as jnp
from jax import lax
from jax.experimental import pallas as pl
from jax.experimental.pallas import tpu as pltpu
from jax.sharding import Mesh, PartitionSpec as P

outer_rate = 0.7
decay_factor = 0.9


def exchange(blocks, along, across, turn):
    n = math.prod(lax.axis_size(a) for a in along)
    places = list(itertools.product(*(range(lax.axis_size(a)) for a in across)))
    groups = [[(k + turn(*at)) % n * len(places) + i for k in range(n)] for i, at in enumerate(places)]
    return lax.all_to_all(blocks, along + across, 0, 0, axis_index_groups=groups, tiled=True)


def spread(block, along, across, turn):
    n = math.prod(lax.axis_size(a) for a in along)
    return exchange(jnp.broadcast_to(block[None], (n,) + block.shape), along, across, turn)


def by_core(c):
    return 2 * c


HBM = pl.BlockSpec(memory_space=pl.ANY)
WHOLE = pl.BlockSpec(memory_space=pltpu.VMEM)
SCALARS = pl.BlockSpec(memory_space=pltpu.SMEM)


def gather_kernel(at, tokens, t1, t3, out, sems):
    part = out.shape[2]
    own = tokens.at[:, pl.ds(pl.multiple_of(at[0] * part, part), part)]
    copies = [pltpu.make_async_copy(source, out.at[i], sems.at[i]) for i, source in enumerate((own, t1, t3))]
    for copy in copies:
        copy.start()
    for copy in copies:
        copy.wait()


def gather_tokens(at, tokens, t1, t3):
    tok, part = t1.shape
    return pl.pallas_call(
        gather_kernel,
        out_shape=jax.ShapeDtypeStruct((3, tok, part), tokens.dtype),
        in_specs=[SCALARS, HBM, HBM, HBM],
        out_specs=WHOLE,
        scratch_shapes=[pltpu.SemaphoreType.DMA((3,))],
        compiler_params=pltpu.CompilerParams(vmem_limit_bytes=16 * 2**20),
        cost_estimate=pl.CostEstimate(flops=0, bytes_accessed=2**26, transcendentals=0),
    )(at, *(pltpu.with_memory_space_constraint(p, pltpu.HBM) for p in (tokens, t1, t3)))


def load(at, core, rows_y, near, far0, far1, w, t, sem_w, sem_t):
    nl, nh, nzl = rows_y.shape[:3]
    nx, tok, width = t.shape[1:]
    half = tok // 2
    turn = by_core(at[2])
    copies = []
    for h in range(nh):
        columns = pl.ds(pl.multiple_of((2 * h + core) * width, width), width)
        places = [(near.at[i, :, columns], lax.rem(at[0] + 2 * nx - d - turn, nx), pl.ds(0, tok)) for i, d in enumerate((0, 1, 3))]
        opposite = lax.rem(at[0] + 2 * nx - 2 - turn, nx)
        places.append((far0.at[:, columns], opposite, pl.ds(0, half)))
        places.append((far1.at[:, columns], opposite, pl.ds(half, half)))
        mine = [
            pltpu.make_async_copy(source, t.at[h, block, rows], sem_t.at[h, i])
            for i, (source, block, rows) in enumerate(places)
        ]
        for l in range(nl):
            for z in range(nzl):
                place = w.at[h, :, lax.rem(z + by_core(core), nzl), lax.rem(l + core, nl)]
                mine.append(pltpu.make_async_copy(rows_y.at[l, h, z], place, sem_w.at[h, l * nzl + z]))
        for copy in mine:
            copy.start()
        copies.append(mine)
    return copies


def product(h, w, t):
    nx, tok, width = t.shape[1:]
    return jnp.dot(
        t[h].reshape(nx * tok, width), w[h].reshape(width, w.shape[-1]), preferred_element_type=jnp.float32
    )


def first_kernel(at, rows_y, near, far0, far1, total, fresh, w, t, sem_w, sem_t, sem_f):
    copies = load(at, at[2], rows_y, near, far0, far1, w, t, sem_w, sem_t)
    for h, mine in enumerate(copies):
        for copy in mine:
            copy.wait()
        total[...] = product(h, w, t) if h == 0 else total[...] + product(h, w, t)
    back = pltpu.make_async_copy(w.at[at[1]], fresh, sem_f)
    back.start()
    back.wait()


def second_kernel(at, rows_y, near, far0, far1, total, out, w, t, sem_w, sem_t, o, sem_o):
    copies = load(at, 1 - at[2], rows_y, near, far0, far1, w, t, sem_w, sem_t)
    last = len(copies) - 1
    for h, mine in enumerate(copies):
        for copy in mine:
            copy.wait()
        if h < last:
            total[...] += product(h, w, t)
        else:
            o[...] = (total[...] + product(h, w, t)).astype(o.dtype)
    back = pltpu.make_async_copy(o, out, sem_o)
    back.start()
    back.wait()


def multiply(at, rows_y, tokens, total=None):
    nl, nh, nzl, nzh, rows, kv = rows_y.shape
    nx = 4
    tok, part = tokens[0].shape[1:]
    width = part // (2 * nh)
    block = (nzh, nzl, nl, rows, kv)
    common = dict(
        compiler_params=pltpu.CompilerParams(vmem_limit_bytes=16 * 2**20),
        cost_estimate=pl.CostEstimate(
            flops=nx * tok * part * kv, bytes_accessed=4 * 2**20, transcendentals=0
        ),
    )
    scratch = [
        pltpu.VMEM((nh,) + block, jnp.bfloat16),
        pltpu.VMEM((nh, nx, tok, width), jnp.bfloat16),
        pltpu.SemaphoreType.DMA((nh, nl * nzl)),
        pltpu.SemaphoreType.DMA((nh, len(tokens) + 2)),
    ]
    if total is None:
        return pl.pallas_call(
            first_kernel,
            out_shape=(
                jax.ShapeDtypeStruct((nx * tok, kv), jnp.float32),
                jax.ShapeDtypeStruct(block, jnp.bfloat16),
            ),
            in_specs=[SCALARS] + [HBM] * 4,
            out_specs=(WHOLE, HBM),
            scratch_shapes=scratch + [pltpu.SemaphoreType.DMA],
            **common,
        )(at, rows_y, *tokens)
    return pl.pallas_call(
        second_kernel,
        out_shape=jax.ShapeDtypeStruct((nx * tok, kv), jnp.bfloat16),
        in_specs=[SCALARS] + [HBM] * 4 + [WHOLE],
        out_specs=HBM,
        scratch_shapes=scratch + [pltpu.VMEM((nx * tok, kv), jnp.bfloat16), pltpu.SemaphoreType.DMA],
        **common,
    )(at, rows_y, *tokens, total)


def local(tokens, master, momentum, trained):
    nzh, nzl, nl, nx, nh = (lax.axis_size(a) for a in ("zh", "zl", "yl", "x", "yh"))
    rows, kv = master.shape
    tok, depth = tokens.shape
    zh, zl, x, yh, c = (lax.axis_index(a) for a in ("zh", "zl", "x", "yh", "c"))
    part = depth // nx
    replicas = nzh * nzl * nl

    trained = trained[0].reshape(nzh, nzl * nl, rows, kv)
    near = lax.all_to_all(trained, ("zl", "yl"), 1, 1, tiled=True)
    near = jnp.sum(near.astype(jnp.float32), axis=1)

    start = lax.optimization_barrier(master.astype(jnp.bfloat16)).astype(jnp.float32)
    gain = outer_rate * (1 + decay_factor) / replicas
    base = master - outer_rate * ((1 + decay_factor) * start + decay_factor**2 * momentum)
    mine = (jnp.arange(nzh) == zh)[:, None, None]
    sent = jnp.where(mine, near + base / gain, near).astype(jnp.float16)
    far = spread(sent, ("zh",), ("zl", "c"), lambda zl, c: zl + 2 * c)
    fresh = (gain * jnp.sum(far.astype(jnp.float32), axis=0)).astype(jnp.bfloat16)

    near_own = lax.dynamic_index_in_dim(near, zh, 0, keepdims=False)
    others = lax.dynamic_index_in_dim(far, zh, 1, keepdims=False).astype(jnp.float32)
    from_me = (jnp.arange(nzh) == (zh + 2 * nzh - zl - 2 * c) % nzh)[:, None, None]
    summed = jnp.sum(jnp.where(from_me, near_own[None], others), axis=0)
    pseudo = start - summed / replicas
    new_momentum = decay_factor * momentum + pseudo
    new_master = master - outer_rate * (pseudo + decay_factor * new_momentum)

    at = jnp.stack([x, yh, c]).astype(jnp.int32)
    def piece(d, first=0, count=tok):
        block = lax.dynamic_slice(tokens, (first, (x + d) % nx * part), (count, part))
        return lax.ppermute(block, "x", [(i, (i + d) % nx) for i in range(nx)])

    half = tok // 2
    near_tokens = gather_tokens(at, tokens, piece(1), piece(3))
    far0, far1 = piece(2, 0, half), piece(2, half, half)
    fresh, near_tokens, far0 = lax.optimization_barrier((fresh, near_tokens, far0))

    rows_z = spread(fresh, ("zl",), ("c",), by_core)
    rows_y = spread(rows_z, ("yl", "yh"), ("c",), by_core).reshape(nl, nh, nzl, nzh, rows, kv)
    rows_y, far1, new_master, new_momentum = lax.optimization_barrier((rows_y, far1, new_master, new_momentum))
    other = lax.ppermute(rows_y, "c", [(0, 1), (1, 0)])

    far0, far1 = (pltpu.with_memory_space_constraint(p, pltpu.HBM) for p in (far0, far1))
    taken = (near_tokens, far0, far1)
    total, refreshed = multiply(at, rows_y, taken)
    share = multiply(at, other, taken, total).reshape(nx, tok, kv)
    share = exchange(share, ("x",), ("c",), by_core)
    key_values = jnp.sum(share.astype(jnp.float32), axis=0)
    return (new_master, new_momentum, refreshed.reshape(-1, kv), key_values)


def solution(mesh):
    fine = Mesh(mesh.devices.reshape(4, 4, 2, 4, 2, 2), ("zh", "zl", "yl", "x", "yh", "c"))
    replica, fsdp = ("zh", "zl", "yl"), ("x", "yh", "c")
    in_specs = (
        P(replica + fsdp, None),
        P(fsdp + replica, None),
        P(fsdp + replica, None),
        P(replica, fsdp, None),
    )
    out_specs = (
        P(fsdp + replica, None),
        P(fsdp + replica, None),
        P(fsdp, None),
        P(replica + fsdp, None),
    )
    return jax.shard_map(local, mesh=fine, in_specs=in_specs, out_specs=out_specs, check_vma=False)
```

time: 323 us -> 108 us (0.33)
  waiting for transfers between devices: 244 us -> 13.1 us
  starting transfers between devices: 0.08 us -> 49.8 us
  blocking collectives: 53.2 us -> 21.6 us
  between operations: 14 us -> 0.87 us
  local copies, waits for them, and re-layouts: 0.81 us -> 9.57 us
  Pallas kernels: 0 us -> 8.37 us
  matrix products: 5.97 us -> 0 us
    all_gather x1 -> x0, waiting for transfers between devices: 126 us -> none  [local(): lax.all_gather(refreshed, 'fsdp', axis=0, tiled=True)]
    reduce_scatter x1 -> x0, waiting for transfers between devices: 118 us -> none  [local(): lax.psum_scatter(local_shard, 'replica', scatter_dimension=0, tiled=True)]
    all_gather x1 -> x0, blocking collectives: 53.2 us -> none  [local(): lax.all_gather(new_master.astype(jnp.bfloat16), 'replica', axis=0, tiled=...]
    all_to_all x0 -> x3, starting transfers between devices: none -> 30.1 us  [the longest x2 22.7 us: exchange(): lax.all_to_all(blocks, along + across, 0, 0, axis_index_groups=groups, ti...]
    all_to_all x0 -> x2, blocking collectives: none -> 21.6 us  [exchange(): lax.all_to_all(blocks, along + across, 0, 0, axis_index_groups=groups, ti...]
    ppermute x0 -> x5, starting transfers between devices: none -> 19.7 us  [the longest x4 15.6 us: piece(): return lax.ppermute(block, 'x', [(i, (i + d) % nx) for i in range(nx)])]
    ppermute x0 -> x5, waiting for transfers between devices: none -> 10.3 us  [the longest x4 10.3 us: piece(): return lax.ppermute(block, 'x', [(i, (i + d) % nx) for i in range(nx)])]
    pallas_call x0 -> x3, Pallas kernels: none -> 8.37 us  [the longest x1 3.13 us: multiply(): pl.pallas_call(first_kernel, out_shape=(jax.ShapeDtypeStruct((nx * tok, k...]
  transfers between devices with their start and end apart: 2 -> 8, of which waited for: 2 -> 4; matrix products, arithmetic and copies ran while one was open for 0% -> 7% of each run, Pallas kernels for 0% -> 5%
where the time goes in v2:
time: 108 us; the launch traced here: 107 us
  starting transfers between devices  49.8 us (46%)
  blocking collectives  21.6 us (20%)
  waiting for transfers between devices  13.1 us (12%)
  local copies, waits for them, and re-layouts  9.57 us (9%)
  Pallas kernels  8.37 us (8%)
  other arithmetic  3.53 us (3%)
    all_to_all x2, starting transfers between devices, exchange(): lax.all_to_all(blocks, along + across, 0, 0, axis_index_groups=groups, ti...  22.7 us
    all_to_all x2, blocking collectives, exchange(): lax.all_to_all(blocks, along + across, 0, 0, axis_index_groups=groups, ti...  21.6 us
    ppermute x4, starting transfers between devices, piece(): return lax.ppermute(block, 'x', [(i, (i + d) % nx) for i in range(nx)])  15.6 us
    ppermute x4, waiting for transfers between devices, piece(): return lax.ppermute(block, 'x', [(i, (i + d) % nx) for i in range(nx)])  10.3 us
    all_to_all x1, starting transfers between devices, local(): near = lax.all_to_all(trained, ('zl', 'yl'), 1, 1, tiled=True)  7.46 us
    dynamic_slice x2, local copies, waits for them, and re-layouts, piece(): lax.dynamic_slice(tokens, (first, (x + d) % nx * part), (count, part))  4.35 us
    ppermute x1, starting transfers between devices, local(): other = lax.ppermute(rows_y, 'c', [(0, 1), (1, 0)])  4.13 us
    pallas_call x1, Pallas kernels, multiply(): pl.pallas_call(first_kernel, out_shape=(jax.ShapeDtypeStruct((nx * tok, k...  3.13 us
  transfers between devices with their start and end apart: 8, of which 4 were waited for; matrix products, arithmetic and copies ran while one was open for 7% of the time, Pallas kernels for 5%

profile of v2, /device:TPU:1, one launch (start us, length us, event | category | flops | bytes accessed | tf_op | source)
XLA Modules:
  0.0 106.9 jit_solution(7420875006580122882)
XLA Ops:
  0.6 0.0 copy-start.3
  0.6 0.0 copy-start.5
  0.7 1.9 %copy.11 = bf16[4,8,16,512]{3,2,0,1:T(8,128)(2,1)} copy(bf16[4,8,16,512]{3,2,1,0:T(8,128)(2,1)} %bitcast.15) | data formatting | bytes 1048576 | tf_op jit(solution)/shard_map/reshape;squeeze | solution.py:166
  2.5 7.5 %all-to-all-start = ((bf16[4,8,16,512]{3,2,0,1:T(8,128)(2,1)}), bf16[4,8,16,512]{3,2,0,1:T(8,128)(2,1)S(1)}, u32[]{:S(2)}, u32[]{:S(2)}) async-start(bf16[4,8,16,512]{3,2,0,1:T(8,128)(2,1)} %copy.11), calls=%async_computation | async-start | bytes 1048576 | tf_op jit(solution)/shard_map/all_to_all | solution.py:167
  10.0 2.4 %constant_dynamic-slice_fusion.1 = (bf16[192,2048]{1,0:T(8,128)(2,1)}, bf16[192,2048]{1,0:T(8,128)(2,1)S(1)}) fusion(bf16[192,8192]{1,0:T(8,128)(2,1)} %tokens.1, s32[]{:T(128)S(6)} %select_n.53, s32[]{:T(128)S(6)} %select_n.51), kind=kLoop, calls=%fused_computation.18 | loop fusion | bytes 3145736 | tf_op jit(solution)/shard_map/dynamic_slice | solution.py:188
  12.4 4.4 %collective-permute-start.1 = (bf16[192,2048]{1,0:T(8,128)(2,1)}, bf16[192,2048]{1,0:T(8,128)(2,1)S(1)}, u32[]{:S(2)}, u32[]{:S(2)}) collective-permute-start(bf16[192,2048]{1,0:T(8,128)(2,1)} %get-tuple-element.24), channel_id=1, source_target_pairs={{0,12},{4,0},{8,4},{12,8},{1,13},{5,1},{9,5},{13,9},{2,14},{6,2},{... | collective-permute-start | bytes 2359304 | tf_op jit(solution)/shard_map/ppermute | solution.py:189
  16.8 1.9 %collective-permute-start = (bf16[192,2048]{1,0:T(8,128)(2,1)S(1)}, bf16[192,2048]{1,0:T(8,128)(2,1)}, u32[]{:S(2)}, u32[]{:S(2)}) collective-permute-start(bf16[192,2048]{1,0:T(8,128)(2,1)S(1)} %get-tuple-element.25), channel_id=1, source_target_pairs={{0,4},{4,8},{8,12},{12,0},{1,5},{5,9},{9,13},{13,1},{2,6},{6,10},{... | collective-permute-start | bytes 2359304 | tf_op jit(solution)/shard_map/ppermute | solution.py:189
  18.7 0.0 copy-done.3
  18.8 0.0 copy-start.4
  18.8 0.0 copy-done.5
  18.8 0.5 copy-done.4
  19.4 1.1 %all-to-all-done = bf16[4,8,16,512]{3,2,0,1:T(8,128)(2,1)S(1)} async-done(((bf16[4,8,16,512]{3,2,0,1:T(8,128)(2,1)}), bf16[4,8,16,512]{3,2,0,1:T(8,128)(2,1)S(1)}, u32[]{:S(2)}, u32[]{:S(2)}) %all-to-all-start) | async-done | bytes 524320 | tf_op jit(solution)/shard_map/all_to_all | solution.py:167
  20.5 0.1 convert_reduce_fusion.1
  20.6 0.1 fusion
  20.7 0.7 broadcast_in_dim.33
  21.4 17.1 %all-to-all-start.1 = ((f16[4,4,16,512]{3,2,1,0:T(8,128)(2,1)}), f16[4,4,16,512]{3,2,1,0:T(8,128)(2,1)S(1)}, u32[]{:S(2)}, u32[]{:S(2)}) async-start(f16[4,4,16,512]{3,2,1,0:T(8,128)(2,1)} %broadcast_in_dim.33), calls=%async_computation.1 | async-start | bytes 524288 | tf_op jit(solution)/shard_map/all_to_all | solution.py:19
  38.5 1.9 %constant_dynamic-slice_fusion.3 = (bf16[96,2048]{1,0:T(8,128)(2,1)}, bf16[96,2048]{1,0:T(8,128)(2,1)S(1)}) fusion(bf16[192,8192]{1,0:T(8,128)(2,1)} %tokens.1, s32[]{:T(128)S(6)} %select_n.55), kind=kLoop, calls=%fused_computation.22 | loop fusion | bytes 1572868 | tf_op jit(solution)/shard_map/dynamic_slice | solution.py:188
  40.5 4.6 %collective-permute-start.2 = (bf16[96,2048]{1,0:T(8,128)(2,1)S(1)}, bf16[96,2048]{1,0:T(8,128)(2,1)S(1)}, u32[]{:S(2)}, u32[]{:S(2)}) collective-permute-start(bf16[96,2048]{1,0:T(8,128)(2,1)S(1)} %get-tuple-element.23), channel_id=1, source_target_pairs={{0,8},{4,12},{8,0},{12,4},{1,9},{5,13},{9,1},{13,5},{2,10},{6,14},... | collective-permute-start | bytes 1179656 | tf_op jit(solution)/shard_map/ppermute | solution.py:189
  45.1 0.1 pad_add_fusion.at
  45.2 0.0 collective-permute-done.1.t3
  45.2 0.0 copy-start.2
  45.2 0.9 copy-done.2
  46.1 0.0 collective-permute-done.t1
  46.1 2.2 %shard_map.75.near = bf16[3,192,2048]{2,1,0:T(8,128)(2,1)S(1)} custom-call(s32[3]{0:T(128)S(1)} %pad_add_fusion.at, bf16[192,8192]{1,0:T(8,128)(2,1)} %tokens.1, bf16[192,2048]{1,0:T(8,128)(2,1)} %collective-permute-done.t1, bf16[192,2048]{1,0:T(8,128)(2,1)} %copy-done.2), custom_call_target="tpu_custom_call" | custom-call | bytes 67108864 | tf_op jit(solution)/shard_map/pallas_call | solution.py:48
  48.3 0.0 all-to-all-done.1
  48.3 0.0 copy-start.1
  48.4 6.0 %collective-permute-done.2.far0 = bf16[96,2048]{1,0:T(8,128)(2,1)S(1)} collective-permute-done((bf16[96,2048]{1,0:T(8,128)(2,1)S(1)}, bf16[96,2048]{1,0:T(8,128)(2,1)S(1)}, u32[]{:S(2)}, u32[]{:S(2)}) %collective-permute-start.2) | collective-permute-done | bytes 393248 | tf_op jit(solution)/shard_map/ppermute | solution.py:189
  54.4 0.0 copy-start
  54.4 7.9 %all_to_all.25 = bf16[4,4,16,512]{3,2,1,0:T(8,128)(2,1)S(1)} all-to-all(bf16[4,4,16,512]{3,2,1,0:T(8,128)(2,1)S(1)} %broadcast_in_dim.50), channel_id=1, replica_groups={{0,32,64,96},{65,97,1,33},{2,34,66,98},{67,99,3,35},{4,36,68,100},{69,1..., dimensions={0} | all-to-all | bytes 524288 | tf_op jit(solution)/shard_map/all_to_all | solution.py:19
  62.3 1.1 %broadcast_in_dim.51 = bf16[4,4,4,16,512]{4,3,2,1,0:T(8,128)(2,1)} broadcast(bf16[4,4,16,512]{3,2,1,0:T(8,128)(2,1)S(1)} %all_to_all.25), dimensions={1,2,3,4} | broadcast | bytes 1310720 | tf_op jit(solution)/shard_map/broadcast_in_dim | solution.py:24
  63.4 0.0 copy-done.1
  63.4 0.0 copy-done
  63.4 5.5 %all-to-all-start.3 = ((bf16[4,4,4,16,512]{4,3,2,1,0:T(8,128)(2,1)}), bf16[4,4,4,16,512]{4,3,2,1,0:T(8,128)(2,1)S(1)}, u32[]{:S(2)}, u32[]{:S(2)}) async-start(bf16[4,4,4,16,512]{4,3,2,1,0:T(8,128)(2,1)} %broadcast_in_dim.51), calls=%async_computation.3 | async-start | bytes 2097152 | tf_op jit(solution)/shard_map/all_to_all | solution.py:19
  68.9 4.6 %collective-permute-start.3 = (bf16[96,2048]{1,0:T(8,128)(2,1)}, bf16[96,2048]{1,0:T(8,128)(2,1)}, u32[]{:S(2)}, u32[]{:S(2)}) collective-permute-start(bf16[96,2048]{1,0:T(8,128)(2,1)} %get-tuple-element.22), channel_id=1, source_target_pairs={{0,8},{4,12},{8,0},{12,4},{1,9},{5,13},{9,1},{13,5},{2,10},{6,14},... | collective-permute-start | bytes 1179656 | tf_op jit(solution)/shard_map/ppermute | solution.py:189
  73.6 0.9 fusion.1
  74.6 1.4 %multiply_add_fusion = (f32[16,512]{1,0:T(8,128)}, f32[16,512]{1,0:T(8,128)}) fusion(f32[16,512]{1,0:T(8,128)} %param.6, f32[16,512]{1,0:T(8,128)S(1)} %fusion.1, bf16[16,512]{1,0:T(8,128)(2,1)} %copy-done.4, f32[16,512]{1,0:T(8,128)} %param.5), kind=kLoop, calls=%fused_computation.15 | loop fusion | flops 73728 | bytes 180224 | tf_op jit(solution)/shard_map/add | solution.py:183
  76.0 4.3 %collective-permute-done.3.far1 = bf16[96,2048]{1,0:T(8,128)(2,1)} collective-permute-done((bf16[96,2048]{1,0:T(8,128)(2,1)}, bf16[96,2048]{1,0:T(8,128)(2,1)}, u32[]{:S(2)}, u32[]{:S(2)}) %collective-permute-start.3) | collective-permute-done | bytes 393248 | tf_op jit(solution)/shard_map/ppermute | solution.py:189
  80.3 1.7 %all-to-all-done.3 = bf16[4,4,4,16,512]{4,3,2,1,0:T(8,128)(2,1)S(1)} async-done(((bf16[4,4,4,16,512]{4,3,2,1,0:T(8,128)(2,1)}), bf16[4,4,4,16,512]{4,3,2,1,0:T(8,128)(2,1)S(1)}, u32[]{:S(2)}, u32[]{:S(2)}) %all-to-all-start.3) | async-done | bytes 1048608 | tf_op jit(solution)/shard_map/all_to_all | solution.py:19
  81.9 4.1 %collective-permute-start.4 = (bf16[2,2,4,4,16,512]{5,4,3,2,1,0:T(8,128)(2,1)S(1)}, bf16[2,2,4,4,16,512]{5,4,3,2,1,0:T(8,128)(2,1)S(1)}, u32[]{:S(2)}, u32[]{:S(2)}) collective-permute-start(bf16[2,2,4,4,16,512]{5,4,3,2,1,0:T(8,128)(2,1)S(1)} %bitcast.12), channel_id=1, source_target_pairs={{0,1},{1,0},{2,3},{3,2},{4,5},{5,4},{6,7},{7,6},{8,9},{9,8},{10,11... | collective-permute-start | bytes 3145736 | tf_op jit(solution)/shard_map/ppermute | solution.py:199
  86.1 3.1 %shard_map.76 = (f32[768,512]{1,0:T(8,128)S(1)}, bf16[4,4,2,16,512]{4,3,2,1,0:T(8,128)(2,1)}) custom-call(s32[3]{0:T(128)S(1)} %pad_add_fusion.at, bf16[2,2,4,4,16,512]{5,4,3,2,1,0:T(8,128)(2,1)S(1)} %bitcast.13, bf16[3,192,2048]{2,1,0:T(8,128)(2,1)S(1)} %shard_map.75.near, bf16[96,2048]{1,0:T(8,128)(2,1)} %copy-done, ...), custom_call_target="tpu_custom_call" | custom-call | flops 805306368 | bytes 4194304 | tf_op jit(solution)/shard_map/pallas_call | solution.py:137
  89.2 0.0 collective-permute-done.4.rows_y
  89.2 3.1 %shard_map.77 = bf16[768,512]{1,0:T(8,128)(2,1)S(1)} custom-call(s32[3]{0:T(128)S(1)} %pad_add_fusion.at, bf16[2,2,4,4,16,512]{5,4,3,2,1,0:T(8,128)(2,1)S(1)} %collective-permute-done.4.rows_y, bf16[3,192,2048]{2,1,0:T(8,128)(2,1)S(1)} %shard_map.75.near, bf16[96,2048]{1,0:T(8,128)(2,1)} %copy-done, bf16[96,2048]{1,0:T(8,128)(2,1)} %collective-permute-done.3.far1, ...), custom_call_target="tpu_custom_call" | custom-call | flops 805306368 | bytes 4194304 | tf_op jit(solution)/shard_map/pallas_call | solution.py:148
  92.3 13.7 %all_to_all.26 = bf16[4,192,512]{2,1,0:T(8,128)(2,1)S(1)} all-to-all(bf16[4,192,512]{2,1,0:T(8,128)(2,1)S(1)} %bitcast.14), channel_id=1, replica_groups={{0,4,8,12},{9,13,1,5},{2,6,10,14},{11,15,3,7},{16,20,24,28},{25,29,17,2..., dimensions={0} | all-to-all | bytes 1572864 | tf_op jit(solution)/shard_map/all_to_all | solution.py:19
  106.0 0.9 convert_reduce_fusion
  (8 shorter events, 0.1 us)
Async XLA Ops:
  0.6 18.1 %copy-start.3 = (f32[16,512]{1,0:T(8,128)S(1)}, f32[16,512]{1,0:T(8,128)}, u32[]{:S(2)}) copy-start(f32[16,512]{1,0:T(8,128)} %param.5) | copy-start | bytes 98308
  0.6 18.1 %copy-start.5 = (f32[16,512]{1,0:T(8,128)S(1)}, f32[16,512]{1,0:T(8,128)}, u32[]{:S(2)}) copy-start(f32[16,512]{1,0:T(8,128)} %param.6) | copy-start | bytes 98308
  2.5 18.0 %all-to-all-start = ((bf16[4,8,16,512]{3,2,0,1:T(8,128)(2,1)}), bf16[4,8,16,512]{3,2,0,1:T(8,128)(2,1)S(1)}, u32[]{:S(2)}, u32[]{:S(2)}) async-start(bf16[4,8,16,512]{3,2,0,1:T(8,128)(2,1)} %copy.11), calls=%async_computation | async-start | bytes 1048576 | tf_op jit(solution)/shard_map/all_to_all | solution.py:167
  12.4 32.8 %collective-permute-start.1 = (bf16[192,2048]{1,0:T(8,128)(2,1)}, bf16[192,2048]{1,0:T(8,128)(2,1)S(1)}, u32[]{:S(2)}, u32[]{:S(2)}) collective-permute-start(bf16[192,2048]{1,0:T(8,128)(2,1)} %get-tuple-element.24), channel_id=1, source_target_pairs={{0,12},{4,0},{8,4},{12,8},{1,13},{5,1},{9,5},{13,9},{2,14},{6,2},{... | collective-permute-start | bytes 2359304 | tf_op jit(solution)/shard_map/ppermute | solution.py:189
  16.8 29.3 %collective-permute-start = (bf16[192,2048]{1,0:T(8,128)(2,1)S(1)}, bf16[192,2048]{1,0:T(8,128)(2,1)}, u32[]{:S(2)}, u32[]{:S(2)}) collective-permute-start(bf16[192,2048]{1,0:T(8,128)(2,1)S(1)} %get-tuple-element.25), channel_id=1, source_target_pairs={{0,4},{4,8},{8,12},{12,0},{1,5},{5,9},{9,13},{13,1},{2,6},{6,10},{... | collective-permute-start | bytes 2359304 | tf_op jit(solution)/shard_map/ppermute | solution.py:189
  18.8 0.6 copy-start.4
  21.4 26.9 %all-to-all-start.1 = ((f16[4,4,16,512]{3,2,1,0:T(8,128)(2,1)}), f16[4,4,16,512]{3,2,1,0:T(8,128)(2,1)S(1)}, u32[]{:S(2)}, u32[]{:S(2)}) async-start(f16[4,4,16,512]{3,2,1,0:T(8,128)(2,1)} %broadcast_in_dim.33), calls=%async_computation.1 | async-start | bytes 524288 | tf_op jit(solution)/shard_map/all_to_all | solution.py:19
  40.5 13.9 %collective-permute-start.2 = (bf16[96,2048]{1,0:T(8,128)(2,1)S(1)}, bf16[96,2048]{1,0:T(8,128)(2,1)S(1)}, u32[]{:S(2)}, u32[]{:S(2)}) collective-permute-start(bf16[96,2048]{1,0:T(8,128)(2,1)S(1)} %get-tuple-element.23), channel_id=1, source_target_pairs={{0,8},{4,12},{8,0},{12,4},{1,9},{5,13},{9,1},{13,5},{2,10},{6,14},... | collective-permute-start | bytes 1179656 | tf_op jit(solution)/shard_map/ppermute | solution.py:189
  45.2 0.9 copy-start.2
  48.3 15.1 %copy-start.1 = (f16[4,4,16,512]{3,2,1,0:T(8,128)(2,1)}, f16[4,4,16,512]{3,2,1,0:T(8,128)(2,1)S(1)}, u32[]{:S(2)}) copy-start(f16[4,4,16,512]{3,2,1,0:T(8,128)(2,1)S(1)} %all-to-all-done.1) | copy-start | bytes 786436
  54.4 9.0 %copy-start = (bf16[96,2048]{1,0:T(8,128)(2,1)}, bf16[96,2048]{1,0:T(8,128)(2,1)S(1)}, u32[]{:S(2)}) copy-start(bf16[96,2048]{1,0:T(8,128)(2,1)S(1)} %collective-permute-done.2.far0) | copy-start | bytes 1179652
  63.4 18.5 %all-to-all-start.3 = ((bf16[4,4,4,16,512]{4,3,2,1,0:T(8,128)(2,1)}), bf16[4,4,4,16,512]{4,3,2,1,0:T(8,128)(2,1)S(1)}, u32[]{:S(2)}, u32[]{:S(2)}) async-start(bf16[4,4,4,16,512]{4,3,2,1,0:T(8,128)(2,1)} %broadcast_in_dim.51), calls=%async_computation.3 | async-start | bytes 2097152 | tf_op jit(solution)/shard_map/all_to_all | solution.py:19
  68.9 11.3 %collective-permute-start.3 = (bf16[96,2048]{1,0:T(8,128)(2,1)}, bf16[96,2048]{1,0:T(8,128)(2,1)}, u32[]{:S(2)}, u32[]{:S(2)}) collective-permute-start(bf16[96,2048]{1,0:T(8,128)(2,1)} %get-tuple-element.22), channel_id=1, source_target_pairs={{0,8},{4,12},{8,0},{12,4},{1,9},{5,13},{9,1},{13,5},{2,10},{6,14},... | collective-permute-start | bytes 1179656 | tf_op jit(solution)/shard_map/ppermute | solution.py:189
  81.9 7.3 %collective-permute-start.4 = (bf16[2,2,4,4,16,512]{5,4,3,2,1,0:T(8,128)(2,1)S(1)}, bf16[2,2,4,4,16,512]{5,4,3,2,1,0:T(8,128)(2,1)S(1)}, u32[]{:S(2)}, u32[]{:S(2)}) collective-permute-start(bf16[2,2,4,4,16,512]{5,4,3,2,1,0:T(8,128)(2,1)S(1)} %bitcast.12), channel_id=1, source_target_pairs={{0,1},{1,0},{2,3},{3,2},{4,5},{5,4},{6,7},{7,6},{8,9},{9,8},{10,11... | collective-permute-start | bytes 3145736 | tf_op jit(solution)/shard_map/ppermute | solution.py:199

commit v3 on v0

v3 whole, which is shorter than its diff:
```python
import itertools
import math

import jax
import jax.numpy as jnp
from jax import lax
from jax.experimental import pallas as pl
from jax.experimental.pallas import tpu as pltpu
from jax.sharding import Mesh, PartitionSpec as P

REPLICAS = 32
outer_rate = 0.7
decay_factor = 0.9


def exchange(blocks, along, across, turn):
    n = math.prod(lax.axis_size(a) for a in along)
    places = list(itertools.product(*(range(lax.axis_size(a)) for a in across)))
    groups = [[(k + turn(*at)) % n * len(places) + i for k in range(n)] for i, at in enumerate(places)]
    return lax.all_to_all(blocks, along + across, 0, 0, axis_index_groups=groups, tiled=True)


def exchange(blocks, along, across, turn):
    n = math.prod(lax.axis_size(a) for a in along)
    places = list(itertools.product(*(range(lax.axis_size(a)) for a in across)))
    groups = [[(k + turn(*at)) % n * len(places) + i for k in range(n)] for i, at in enumerate(places)]
    return lax.all_to_all(blocks, along + across, 0, 0, axis_index_groups=groups, tiled=True)


def exchange(blocks, along, across, turn):
    n = math.prod(lax.axis_size(a) for a in along)
    places = list(itertools.product(*(range(lax.axis_size(a)) for a in across)))
    groups = [[(k + turn(*at)) % n * len(places) + i for k in range(n)] for i, at in enumerate(places)]
    return lax.all_to_all(blocks, along + across, 0, 0, axis_index_groups=groups, tiled=True)


def exchange(blocks, along, across, turn):
    n = math.prod(lax.axis_size(a) for a in along)
    places = list(itertools.product(*(range(lax.axis_size(a)) for a in across)))
    groups = [[(k + turn(*at)) % n * len(places) + i for k in range(n)] for i, at in enumerate(places)]
    return lax.all_to_all(blocks, along + across, 0, 0, axis_index_groups=groups, tiled=True)


def exchange(blocks, along, across, turn):
    n = math.prod(lax.axis_size(a) for a in along)
    places = list(itertools.product(*(range(lax.axis_size(a)) for a in across)))
    groups = [[(k + turn(*at)) % n * len(places) + i for k in range(n)] for i, at in enumerate(places)]
    return lax.all_to_all(blocks, along + across, 0, 0, axis_index_groups=groups, tiled=True)


def exchange(blocks, along, across, turn):
    n = math.prod(lax.axis_size(a) for a in along)
    places = list(itertools.product(*(range(lax.axis_size(a)) for a in across)))
    groups = [[(k + turn(*at)) % n * len(places) + i for k in range(n)] for i, at in enumerate(places)]
    return lax.all_to_all(blocks, along + across, 0, 0, axis_index_groups=groups, tiled=True)


def exchange(blocks, along, across, turn):
    n = math.prod(lax.axis_size(a) for a in along)
    places = list(itertools.product(*(range(lax.axis_size(a)) for a in across)))
    groups = [[(k + turn(*at)) % n * len(places) + i for k in range(n)] for i, at in enumerate(places)]
    return lax.all_to_all(blocks, along + across, 0, 0, axis_index_groups=groups, tiled=True)


def exchange(blocks, along, across, turn):
    n = math.prod(lax.axis_size(a) for a in along)
    places = list(itertools.product(*(range(lax.axis_size(a)) for a in across)))
    groups = [[(k + turn(*at)) % n * len(places) + i for k in range(n)] for i, at in enumerate(places)]
    return lax.all_to_all(blocks, along + across, 0, 0, axis_index_groups=groups, tiled=True)


def exchange(blocks, along, across, turn):
    n = math.prod(lax.axis_size(a) for a in along)
    places = list(itertools.product(*(range(lax.axis_size(a)) for a in across)))
    groups = [[(k + turn(*at)) % n * len(places) + i for k in range(n)] for i, at in enumerate(places)]
    return lax.all_to_all(blocks, along + across, 0, 0, axis_index_groups=groups, tiled=True)


def exchange(blocks, along, across, turn):
    n = math.prod(lax.axis_size(a) for a in along)
    places = list(itertools.product(*(range(lax.axis_size(a)) for a in across)))
    groups = [[(k + turn(*at)) % n * len(places) + i for k in range(n)] for i, at in enumerate(places)]
    return lax.all_to_all(blocks, along + across, 0, 0, axis_index_groups=groups, tiled=True)


def exchange(blocks, along, across, turn):
    n = math.prod(lax.axis_size(a) for a in along)
    places = list(itertools.product(*(range(lax.axis_size(a)) for a in across)))
    groups = [[(k + turn(*at)) % n * len(places) + i for k in range(n)] for i, at in enumerate(places)]
    return lax.all_to_all(blocks, along + across, 0, 0, axis_index_groups=groups, tiled=True)


def exchange(blocks, along, across, turn):
    n = math.prod(lax.axis_size(a) for a in along)
    places = list(itertools.product(*(range(lax.axis_size(a)) for a in across)))
    groups = [[(k + turn(*at)) % n * len(places) + i for k in range(n)] for i, at in enumerate(places)]
    return lax.all_to_all(blocks, along + across, 0, 0, axis_index_groups=groups, tiled=True)


def exchange(blocks, along, across, turn):
    n = math.prod(lax.axis_size(a) for a in along)
    places = list(itertools.product(*(range(lax.axis_size(a)) for a in across)))
    groups = [[(k + turn(*at)) % n * len(places) + i for k in range(n)] for i, at in enumerate(places)]
    return lax.all_to_all(blocks, along + across, 0, 0, axis_index_groups=groups, tiled=True)


def exchange(blocks, along, across, turn):
    n = math.prod(lax.axis_size(a) for a in along)
    places = list(itertools.product(*(range(lax.axis_size(a)) for a in across)))
    groups = [[(k + turn(*at)) % n * len(places) + i for k in range(n)] for i, at in enumerate(places)]
    return lax.all_to_all(blocks, along + across, 0, 0, axis_index_groups=groups, tiled=True)


def spread(block, along, across, turn):
    n = math.prod(lax.axis_size(a) for a in along)
    return exchange(jnp.broadcast_to(block[None], (n,) + block.shape), along, across, turn)


def by_core(c):
    return 2 * c


HBM = pl.BlockSpec(memory_space=pl.ANY)
WHOLE = pl.BlockSpec(memory_space=pltpu.VMEM)
SCALARS = pl.BlockSpec(memory_space=pltpu.SMEM)
LIMIT = pltpu.CompilerParams(vmem_limit_bytes=16 * 2**20)
STEPS = (0, 1, 3, 2)


def gather_kernel(at, tokens, t1, t3, out, sems):
    part = out.shape[2]
    own = tokens.at[:, pl.ds(pl.multiple_of(at[0] * part, part), part)]
    copies = [
        pltpu.make_async_copy(source, out.at[i], sems.at[i]) for i, source in enumerate((own, t1, t3))
    ]
    for copy in copies:
        copy.start()
    for copy in copies:
        copy.wait()


def gather_tokens(at, tokens, t1, t3):
    tok, part = t1.shape
    return pl.pallas_call(
        gather_kernel,
        out_shape=jax.ShapeDtypeStruct((3, tok, part), tokens.dtype),
        in_specs=[SCALARS, HBM, HBM, HBM],
        out_specs=WHOLE,
        scratch_shapes=[pltpu.SemaphoreType.DMA((3,))],
        compiler_params=LIMIT,
        cost_estimate=pl.CostEstimate(flops=0, bytes_accessed=2**26, transcendentals=0),
    )(at, *(pltpu.with_memory_space_constraint(p, pltpu.HBM) for p in (tokens, t1, t3)))


def fetch(sources, places, sems):
    copies = [pltpu.make_async_copy(s, p, sems.at[i]) for i, (s, p) in enumerate(zip(sources, places))]
    for copy in copies:
        copy.start()
    return copies


def parts_of(ref, first):
    cut = first.shape[0]
    return [ref.at[pl.ds(0, cut)], ref.at[pl.ds(cut, ref.shape[0] - cut)]]


def product(core, rows_y, near, far, far_copies):
    nl, nh, nzl, nzh, rows, kv = rows_y.shape
    part = near.shape[2]
    width = part // (2 * nh)
    weights, columns = [], []
    for h in range(nh):
        weights.append(
            jnp.concatenate(
                [
                    rows_y[lax.rem(l + core, nl), h, lax.rem(z + by_core(core), nzl), zh]
                    for zh in range(nzh)
                    for z in range(nzl)
                    for l in range(nl)
                ],
                axis=0,
            )
        )
        columns.append(pl.ds(pl.multiple_of((2 * h + core) * width, width), width))
    right = jnp.concatenate(weights, axis=0)

    def times(blocks):
        left = [jnp.concatenate([block[:, cols] for block in blocks], axis=0) for cols in columns]
        return jnp.dot(jnp.concatenate(left, axis=1), right, preferred_element_type=jnp.float32)

    first = times([near.at[i] for i in range(near.shape[0])])
    for copy in far_copies:
        copy.wait()
    return jnp.concatenate([first, times([far])], axis=0), weights


def first_kernel(at, rows_y, near, far0, far1, total, fresh, w, far, sems, sem):
    copies = fetch((far0, far1), parts_of(far, far0), sems)
    result, weights = product(at[2], rows_y, near, far, copies)
    for h, block in enumerate(weights):
        w[h] = block
    back = pltpu.make_async_copy(w.at[at[1]], fresh, sem)
    back.start()
    total[...] = result
    back.wait()


def second_kernel(at, rows_y, near, far0, far1, total, out, far_here, sems):
    copies = fetch((far0, far1), parts_of(far_here, far0), sems)
    result, _ = product(1 - at[2], rows_y, near, far_here, copies)
    result = result + total[...]
    nx, tok = out.shape[:2]
    for i, step in enumerate(STEPS):
        place = lax.rem(at[0] + 2 * nx - step - by_core(at[2]), nx)
        out[place] = result[i * tok : (i + 1) * tok].astype(out.dtype)


def cost(near, kv):
    tok, part = near.shape[1:]
    return pl.CostEstimate(flops=4 * tok * part * kv, bytes_accessed=4 * 2**20, transcendentals=0)


def pinned(*arrays):
    return [pltpu.with_memory_space_constraint(a, pltpu.HBM) for a in arrays]


def first_product(at, rows_y, near, far0, far1):
    nl, nh, nzl, nzh, rows, kv = rows_y.shape
    tok, part = near.shape[1:]
    deep = nzh * nzl * nl * rows
    return pl.pallas_call(
        first_kernel,
        out_shape=(
            jax.ShapeDtypeStruct((4 * tok, kv), jnp.float32),
            jax.ShapeDtypeStruct((deep, kv), jnp.bfloat16),
        ),
        in_specs=[SCALARS, WHOLE, WHOLE, HBM, HBM],
        out_specs=(WHOLE, HBM),
        scratch_shapes=[
            pltpu.VMEM((nh, deep, kv), jnp.bfloat16),
            pltpu.VMEM((tok, part), near.dtype),
            pltpu.SemaphoreType.DMA((2,)),
            pltpu.SemaphoreType.DMA,
        ],
        compiler_params=LIMIT,
        cost_estimate=cost(near, kv),
    )(at, rows_y, near, *pinned(far0, far1))


def second_product(at, rows_y, near, far0, far1, total):
    kv = rows_y.shape[-1]
    tok, part = near.shape[1:]
    return pl.pallas_call(
        second_kernel,
        out_shape=jax.ShapeDtypeStruct((4, tok, kv), jnp.bfloat16),
        in_specs=[SCALARS, WHOLE, WHOLE, HBM, HBM, WHOLE],
        out_specs=WHOLE,
        scratch_shapes=[pltpu.VMEM((tok, part), near.dtype), pltpu.SemaphoreType.DMA((2,))],
        compiler_params=LIMIT,
        cost_estimate=cost(near, kv),
    )(at, rows_y, near, *pinned(far0, far1), total)


def local(tokens, master, momentum, trained):
    nzh, nzl, nl, nx, nh = (lax.axis_size(a) for a in ("zh", "zl", "yl", "x", "yh"))
    rows, kv = master.shape
    tok, depth = tokens.shape
    zh, x, yh, c = (lax.axis_index(a) for a in ("zh", "x", "yh", "c"))
    at = jnp.stack([x, yh, c, zh]).astype(jnp.int32)
    part = depth // nx

    trained = trained[0].reshape(nzh, nzl * nl, rows, kv)
    near = lax.all_to_all(trained, ("zl", "yl"), 1, 1, tiled=True)
    near = jnp.sum(near.astype(jnp.float32), axis=1)

    start = lax.optimization_barrier(master.astype(jnp.bfloat16))
    gain = outer_rate * (1 + decay_factor) / REPLICAS
    base = master - outer_rate * ((1 + decay_factor) * start.astype(jnp.float32) + decay_factor**2 * momentum)
    offset = base / gain
    mine = (jnp.arange(nzh) == zh)[:, None, None]
    sent = jnp.where(mine, near + offset, near).astype(jnp.float16)
    sums = spread(sent, ("zh",), ("zl", "c"), lambda zl, c: 3)
    sums = jnp.sum(sums.astype(jnp.float32), axis=0)
    fresh = (gain * sums).astype(jnp.bfloat16)

    most = tok // 2
    cuts = [lax.dynamic_slice(tokens, (0, (x + d) % nx * part), (tok, part)) for d in (1, 3, 2)]
    cuts = lax.optimization_barrier(cuts)
    cuts[2:] = lax.optimization_barrier([cuts[2][:most], cuts[2][most:]])
    t1, t3, t20, t21 = (
        lax.ppermute(cut, "x", [(i, (i + d) % nx) for i in range(nx)])
        for d, cut in ((1, cuts[0]), (3, cuts[1]), (2, cuts[2]), (2, cuts[3]))
    )
    near_tokens = gather_tokens(at, tokens, t1, t3)
    fresh, near_tokens, t20 = lax.optimization_barrier((fresh, near_tokens, t20))

    rows_z = spread(fresh, ("zl",), ("c",), by_core)
    rows_y = spread(rows_z, ("yl", "yh"), ("c",), by_core).reshape(nl, nh, nzl, nzh, rows, kv)
    summed = lax.dynamic_index_in_dim(sums, zh, 0, keepdims=False) - offset
    pseudo = start.astype(jnp.float32) - summed / REPLICAS
    new_momentum = decay_factor * momentum + pseudo
    new_master = master - outer_rate * (pseudo + decay_factor * new_momentum)
    rows_y, t21, new_master, new_momentum = lax.optimization_barrier((rows_y, t21, new_master, new_momentum))
    taken = (near_tokens, t20, t21)
    other = lax.ppermute(rows_y, "c", [(0, 1), (1, 0)])

    total, refreshed = first_product(at, rows_y, *taken)
    share = second_product(at, other, *taken, total)
    share = exchange(share, ("x",), ("c",), by_core)
    key_values = jnp.sum(share.astype(jnp.float32), axis=0)
    return (new_master, new_momentum, refreshed, key_values)


def solution(mesh):
    fine = Mesh(mesh.devices.reshape(4, 4, 2, 4, 2, 2), ("zh", "zl", "yl", "x", "yh", "c"))
    replica, fsdp = ("zh", "zl", "yl"), ("x", "yh", "c")
    in_specs = (
        P(replica + fsdp, None),
        P(fsdp + replica, None),
        P(fsdp + replica, None),
        P(replica, fsdp, None),
    )
    out_specs = (
        P(fsdp + replica, None),
        P(fsdp + replica, None),
        P(fsdp, None),
        P(replica + fsdp, None),
    )
    return jax.shard_map(local, mesh=fine, in_specs=in_specs, out_specs=out_specs, check_vma=False)
```

time: 323 us -> 105 us (0.33)
  waiting for transfers between devices: 244 us -> 8.63 us
  starting transfers between devices: 0.08 us -> 52.7 us
  blocking collectives: 53.2 us -> 22.3 us
  between operations: 14 us -> 0.81 us
  local copies, waits for them, and re-layouts: 0.81 us -> 8.99 us
  Pallas kernels: 0 us -> 7.45 us
  matrix products: 5.97 us -> 0 us
    all_gather x1 -> x0, waiting for transfers between devices: 126 us -> none  [local(): lax.all_gather(refreshed, 'fsdp', axis=0, tiled=True)]
    reduce_scatter x1 -> x0, waiting for transfers between devices: 118 us -> none  [local(): lax.psum_scatter(local_shard, 'replica', scatter_dimension=0, tiled=True)]
    all_gather x1 -> x0, blocking collectives: 53.2 us -> none  [local(): lax.all_gather(new_master.astype(jnp.bfloat16), 'replica', axis=0, tiled=...]
    all_to_all x0 -> x3, starting transfers between devices: none -> 28.9 us  [the longest x2 21.5 us: exchange(): lax.all_to_all(blocks, along + across, 0, 0, axis_index_groups=groups, ti...]
    ppermute x0 -> x5, starting transfers between devices: none -> 23.8 us  [the longest x4 15.6 us: local(): lax.ppermute(cut, 'x', [(i, (i + d) % nx) for i in range(nx)])]
    all_to_all x0 -> x2, blocking collectives: none -> 22.3 us  [exchange(): lax.all_to_all(blocks, along + across, 0, 0, axis_index_groups=groups, ti...]
    ppermute x0 -> x5, waiting for transfers between devices: none -> 8.28 us  [the longest x4 8.27 us: local(): lax.ppermute(cut, 'x', [(i, (i + d) % nx) for i in range(nx)])]
    pallas_call x0 -> x3, Pallas kernels: none -> 7.45 us  [the longest x1 2.92 us: first_product(): pl.pallas_call(first_kernel, out_shape=(jax.ShapeDtypeStruct((4 * tok, kv...]
  transfers between devices with their start and end apart: 2 -> 8, of which waited for: 2 -> 3; matrix products, arithmetic and copies ran while one was open for 0% -> 6% of each run, Pallas kernels for 0% -> 5%
where the time goes in v3:
time: 105 us; the launch traced here: 104 us
  starting transfers between devices  52.7 us (50%)
  blocking collectives  22.3 us (21%)
  local copies, waits for them, and re-layouts  8.99 us (9%)
  waiting for transfers between devices  8.63 us (8%)
  Pallas kernels  7.45 us (7%)
  other arithmetic  2.61 us (2%)
    all_to_all x2, blocking collectives, exchange(): lax.all_to_all(blocks, along + across, 0, 0, axis_index_groups=groups, ti...  22.3 us
    all_to_all x2, starting transfers between devices, exchange(): lax.all_to_all(blocks, along + across, 0, 0, axis_index_groups=groups, ti...  21.5 us
    ppermute x4, starting transfers between devices, local(): lax.ppermute(cut, 'x', [(i, (i + d) % nx) for i in range(nx)])  15.6 us
    ppermute x4, waiting for transfers between devices, local(): lax.ppermute(cut, 'x', [(i, (i + d) % nx) for i in range(nx)])  8.27 us
    ppermute x1, starting transfers between devices, local(): other = lax.ppermute(rows_y, 'c', [(0, 1), (1, 0)])  8.18 us
    all_to_all x1, starting transfers between devices, local(): near = lax.all_to_all(trained, ('zl', 'yl'), 1, 1, tiled=True)  7.46 us
    dynamic_slice x1, local copies, waits for them, and re-layouts, local(): lax.dynamic_slice(tokens, (0, (x + d) % nx * part), (tok, part))  2.99 us
    pallas_call x1, Pallas kernels, first_product(): pl.pallas_call(first_kernel, out_shape=(jax.ShapeDtypeStruct((4 * tok, kv...  2.92 us
  transfers between devices with their start and end apart: 8, of which 3 were waited for; matrix products, arithmetic and copies ran while one was open for 6% of the time, Pallas kernels for 5%

profile of v3, /device:TPU:1, one launch (start us, length us, event | category | flops | bytes accessed | tf_op | source)
XLA Modules:
  0.0 103.5 jit_solution(10409468757431487347)
XLA Ops:
  0.6 1.9 %copy.9 = bf16[4,8,16,512]{3,2,0,1:T(8,128)(2,1)} copy(bf16[4,8,16,512]{3,2,1,0:T(8,128)(2,1)} %bitcast.20) | data formatting | bytes 1048576 | tf_op jit(solution)/shard_map/reshape;squeeze | solution.py:272
  2.5 7.5 %all-to-all-start = ((bf16[4,8,16,512]{3,2,0,1:T(8,128)(2,1)}), bf16[4,8,16,512]{3,2,0,1:T(8,128)(2,1)S(1)}, u32[]{:S(2)}, u32[]{:S(2)}) async-start(bf16[4,8,16,512]{3,2,0,1:T(8,128)(2,1)} %copy.9), calls=%async_computation | async-start | bytes 1048576 | tf_op jit(solution)/shard_map/all_to_all | solution.py:273
  10.0 0.0 copy-start.2
  10.0 0.0 copy-start.4
  10.0 3.0 %constant_dynamic-slice_fusion = (bf16[192,2048]{1,0:T(8,128)(2,1)S(1)}, bf16[192,2048]{1,0:T(8,128)(2,1)}, bf16[192,2048]{1,0:T(8,128)(2,1)}) fusion(bf16[192,8192]{1,0:T(8,128)(2,1)} %tokens.1, s32[]{:T(128)S(6)} %select_n.42, s32[]{:T(128)S(6)} %select_n.40, s32[]{:T(128)S(6)} %select_n.38), kind=kLoop, calls=%fused_computation.16 | loop fusion | bytes 4718604 | tf_op jit(solution)/shard_map/dynamic_slice | solution.py:287
  13.0 3.1 %collective-permute-start = (bf16[192,2048]{1,0:T(8,128)(2,1)}, bf16[192,2048]{1,0:T(8,128)(2,1)S(1)}, u32[]{:S(2)}, u32[]{:S(2)}) collective-permute-start(bf16[192,2048]{1,0:T(8,128)(2,1)} %get-tuple-element.18), channel_id=1, source_target_pairs={{0,4},{4,8},{8,12},{12,0},{1,5},{5,9},{9,13},{13,1},{2,6},{6,10},{... | collective-permute-start | bytes 2359304 | tf_op jit(solution)/shard_map/ppermute | solution.py:291
  16.1 3.4 %collective-permute-start.1 = (bf16[192,2048]{1,0:T(8,128)(2,1)}, bf16[192,2048]{1,0:T(8,128)(2,1)}, u32[]{:S(2)}, u32[]{:S(2)}) collective-permute-start(bf16[192,2048]{1,0:T(8,128)(2,1)} %get-tuple-element.19), channel_id=1, source_target_pairs={{0,12},{4,0},{8,4},{12,8},{1,13},{5,1},{9,5},{13,9},{2,14},{6,2},{... | collective-permute-start | bytes 2359304 | tf_op jit(solution)/shard_map/ppermute | solution.py:291
  19.5 0.0 copy-done.2
  19.5 0.0 copy-start.3
  19.5 0.6 copy-done.3
  20.1 0.0 copy-done.4
  20.1 0.4 all-to-all-done
  20.5 0.1 convert_reduce_fusion.1
  20.6 0.1 fusion
  20.6 0.7 broadcast_in_dim.15
  21.4 16.3 %all-to-all-start.1 = ((f16[4,4,16,512]{3,2,1,0:T(8,128)(2,1)}), f16[4,4,16,512]{3,2,1,0:T(8,128)(2,1)S(1)}, u32[]{:S(2)}, u32[]{:S(2)}) async-start(f16[4,4,16,512]{3,2,1,0:T(8,128)(2,1)} %broadcast_in_dim.15), calls=%async_computation.1 | async-start | bytes 524288 | tf_op jit(solution)/shard_map/all_to_all | solution.py:111
  37.7 0.8 fusion.6
  38.5 4.5 %collective-permute-start.2 = (bf16[96,2048]{1,0:T(8,128)(2,1)S(1)}, bf16[96,2048]{1,0:T(8,128)(2,1)S(1)}, u32[]{:S(2)}, u32[]{:S(2)}) collective-permute-start(bf16[96,2048]{1,0:T(8,128)(2,1)S(1)} %get-tuple-element.21), channel_id=1, source_target_pairs={{0,8},{4,12},{8,0},{12,4},{1,9},{5,13},{9,1},{13,5},{2,10},{6,14},... | collective-permute-start | bytes 1179656 | tf_op jit(solution)/shard_map/ppermute | solution.py:291
  43.0 0.1 pad_add_fusion.at
  43.1 0.0 collective-permute-done.t1
  43.1 0.0 copy-start.1
  43.1 0.9 copy-done.1
  44.0 0.0 collective-permute-done.1.t3
  44.0 2.2 %shard_map.75.near = bf16[3,192,2048]{2,1,0:T(8,128)(2,1)S(1)} custom-call(s32[4]{0:T(128)S(1)} %pad_add_fusion.at, bf16[192,8192]{1,0:T(8,128)(2,1)} %tokens.1, bf16[192,2048]{1,0:T(8,128)(2,1)} %copy-done.1, bf16[192,2048]{1,0:T(8,128)(2,1)} %collective-permute-done.1.t3), custom_call_target="tpu_custom_call" | custom-call | bytes 67108864 | tf_op jit(solution)/shard_map/pallas_call | solution.py:144
  46.2 0.0 all-to-all-done.1
  46.2 3.8 %collective-permute-done.2.far0 = bf16[96,2048]{1,0:T(8,128)(2,1)S(1)} collective-permute-done((bf16[96,2048]{1,0:T(8,128)(2,1)S(1)}, bf16[96,2048]{1,0:T(8,128)(2,1)S(1)}, u32[]{:S(2)}, u32[]{:S(2)}) %collective-permute-start.2) | collective-permute-done | bytes 393248 | tf_op jit(solution)/shard_map/ppermute | solution.py:291
  50.1 0.0 copy-start
  50.1 8.6 %all_to_all.25 = bf16[4,4,16,512]{3,2,1,0:T(8,128)(2,1)S(1)} all-to-all(bf16[4,4,16,512]{3,2,1,0:T(8,128)(2,1)S(1)} %broadcast_in_dim.16), channel_id=1, replica_groups={{0,32,64,96},{65,97,1,33},{2,34,66,98},{67,99,3,35},{4,36,68,100},{69,1..., dimensions={0} | all-to-all | bytes 524288 | tf_op jit(solution)/shard_map/all_to_all | solution.py:111
  58.7 1.1 %broadcast_in_dim.17 = bf16[4,4,4,16,512]{4,3,2,1,0:T(8,128)(2,1)} broadcast(bf16[4,4,16,512]{3,2,1,0:T(8,128)(2,1)S(1)} %all_to_all.25), dimensions={1,2,3,4} | broadcast | bytes 1310720 | tf_op jit(solution)/shard_map/broadcast_in_dim | solution.py:116
  59.8 0.0 copy-done
  59.8 5.1 %all-to-all-start.3 = ((bf16[4,4,4,16,512]{4,3,2,1,0:T(8,128)(2,1)}), bf16[4,4,4,16,512]{4,3,2,1,0:T(8,128)(2,1)S(1)}, u32[]{:S(2)}, u32[]{:S(2)}) async-start(bf16[4,4,4,16,512]{4,3,2,1,0:T(8,128)(2,1)} %broadcast_in_dim.17), calls=%async_computation.3 | async-start | bytes 2097152 | tf_op jit(solution)/shard_map/all_to_all | solution.py:111
  64.9 4.6 %collective-permute-start.3 = (bf16[96,2048]{1,0:T(8,128)(2,1)}, bf16[96,2048]{1,0:T(8,128)(2,1)}, u32[]{:S(2)}, u32[]{:S(2)}) collective-permute-start(bf16[96,2048]{1,0:T(8,128)(2,1)} %get-tuple-element.23), channel_id=1, source_target_pairs={{0,8},{4,12},{8,0},{12,4},{1,9},{5,13},{9,1},{13,5},{2,10},{6,14},... | collective-permute-start | bytes 1179656 | tf_op jit(solution)/shard_map/ppermute | solution.py:291
  69.6 1.4 %multiply_add_fusion = (f32[16,512]{1,0:T(8,128)}, f32[16,512]{1,0:T(8,128)}) fusion(f32[16,512]{1,0:T(8,128)} %param.6, f32[4,16,512]{2,1,0:T(8,128)S(1)} %convert_reduce_fusion.2, s32[]{:T(128)S(6)} %select_n.43, bf16[16,512]{1,0:T(8,128)(2,1)} %copy-done.3, f32[16,512]{1,0:T(8,128)} %param.5), kind=kLoop, calls=%fused_computation.15 | loop fusion | flops 131072 | bytes 180228 | tf_op jit(solution)/shard_map/add | solution.py:301
  71.0 4.4 %collective-permute-done.3.far1 = bf16[96,2048]{1,0:T(8,128)(2,1)} collective-permute-done((bf16[96,2048]{1,0:T(8,128)(2,1)}, bf16[96,2048]{1,0:T(8,128)(2,1)}, u32[]{:S(2)}, u32[]{:S(2)}) %collective-permute-start.3) | collective-permute-done | bytes 393248 | tf_op jit(solution)/shard_map/ppermute | solution.py:291
  75.4 0.0 all-to-all-done.3
  75.4 8.2 %collective-permute-start.4 = (bf16[2,2,4,4,16,512]{5,4,3,2,1,0:T(8,128)(2,1)S(1)}, bf16[2,2,4,4,16,512]{5,4,3,2,1,0:T(8,128)(2,1)S(1)}, u32[]{:S(2)}, u32[]{:S(2)}) collective-permute-start(bf16[2,2,4,4,16,512]{5,4,3,2,1,0:T(8,128)(2,1)S(1)} %bitcast.18), channel_id=1, source_target_pairs={{0,1},{1,0},{2,3},{3,2},{4,5},{5,4},{6,7},{7,6},{8,9},{9,8},{10,11... | collective-permute-start | bytes 3145736 | tf_op jit(solution)/shard_map/ppermute | solution.py:305
  83.6 2.9 %shard_map.76 = (f32[768,512]{1,0:T(8,128)S(1)}, bf16[512,512]{1,0:T(8,128)(2,1)}) custom-call(s32[4]{0:T(128)S(1)} %pad_add_fusion.at, bf16[2,2,4,4,16,512]{5,4,3,2,1,0:T(8,128)(2,1)S(1)} %bitcast.19, bf16[3,192,2048]{2,1,0:T(8,128)(2,1)S(1)} %shard_map.75.near, bf16[96,2048]{1,0:T(8,128)(2,1)} %copy-done, bf16[96,2048]{1,0:T(8,128)(2,1)} %collective-permute-done.3.far1), custom_call_target="tpu_custom_call" | custom-call | flops 805306368 | bytes 4194304 | tf_op jit(solution)/shard_map/pallas_call | solution.py:231
  86.6 0.0 collective-permute-done.4.rows_y
  86.6 2.4 %shard_map.77 = bf16[4,192,512]{2,1,0:T(8,128)(2,1)S(1)} custom-call(s32[4]{0:T(128)S(1)} %pad_add_fusion.at, bf16[2,2,4,4,16,512]{5,4,3,2,1,0:T(8,128)(2,1)S(1)} %collective-permute-done.4.rows_y, bf16[3,192,2048]{2,1,0:T(8,128)(2,1)S(1)} %shard_map.75.near, bf16[96,2048]{1,0:T(8,128)(2,1)} %copy-done, bf16[96,2048]{1,0:T(8,128)(2,1)} %collective-permute-done.3.far1, ...), custom_call_target="tpu_custom_call" | custom-call | flops 805306368 | bytes 4194304 | tf_op jit(solution)/shard_map/pallas_call | solution.py:253
  88.9 13.7 %all_to_all.26 = bf16[4,192,512]{2,1,0:T(8,128)(2,1)S(1)} all-to-all(bf16[4,192,512]{2,1,0:T(8,128)(2,1)S(1)} %shard_map.77), channel_id=1, replica_groups={{0,4,8,12},{9,13,1,5},{2,6,10,14},{11,15,3,7},{16,20,24,28},{25,29,17,2..., dimensions={0} | all-to-all | bytes 1572864 | tf_op jit(solution)/shard_map/all_to_all | solution.py:111
  102.7 0.9 convert_reduce_fusion
  (6 shorter events, 0.1 us)
Async XLA Ops:
  2.5 18.0 %all-to-all-start = ((bf16[4,8,16,512]{3,2,0,1:T(8,128)(2,1)}), bf16[4,8,16,512]{3,2,0,1:T(8,128)(2,1)S(1)}, u32[]{:S(2)}, u32[]{:S(2)}) async-start(bf16[4,8,16,512]{3,2,0,1:T(8,128)(2,1)} %copy.9), calls=%async_computation | async-start | bytes 1048576 | tf_op jit(solution)/shard_map/all_to_all | solution.py:273
  10.0 9.5 %copy-start.2 = (f32[16,512]{1,0:T(8,128)S(1)}, f32[16,512]{1,0:T(8,128)}, u32[]{:S(2)}) copy-start(f32[16,512]{1,0:T(8,128)} %param.5) | copy-start | bytes 98308
  10.0 10.1 %copy-start.4 = (f32[16,512]{1,0:T(8,128)S(1)}, f32[16,512]{1,0:T(8,128)}, u32[]{:S(2)}) copy-start(f32[16,512]{1,0:T(8,128)} %param.6) | copy-start | bytes 98308
  13.0 30.1 %collective-permute-start = (bf16[192,2048]{1,0:T(8,128)(2,1)}, bf16[192,2048]{1,0:T(8,128)(2,1)S(1)}, u32[]{:S(2)}, u32[]{:S(2)}) collective-permute-start(bf16[192,2048]{1,0:T(8,128)(2,1)} %get-tuple-element.18), channel_id=1, source_target_pairs={{0,4},{4,8},{8,12},{12,0},{1,5},{5,9},{9,13},{13,1},{2,6},{6,10},{... | collective-permute-start | bytes 2359304 | tf_op jit(solution)/shard_map/ppermute | solution.py:291
  16.1 27.9 %collective-permute-start.1 = (bf16[192,2048]{1,0:T(8,128)(2,1)}, bf16[192,2048]{1,0:T(8,128)(2,1)}, u32[]{:S(2)}, u32[]{:S(2)}) collective-permute-start(bf16[192,2048]{1,0:T(8,128)(2,1)} %get-tuple-element.19), channel_id=1, source_target_pairs={{0,12},{4,0},{8,4},{12,8},{1,13},{5,1},{9,5},{13,9},{2,14},{6,2},{... | collective-permute-start | bytes 2359304 | tf_op jit(solution)/shard_map/ppermute | solution.py:291
  19.5 0.6 copy-start.3
  21.4 24.8 %all-to-all-start.1 = ((f16[4,4,16,512]{3,2,1,0:T(8,128)(2,1)}), f16[4,4,16,512]{3,2,1,0:T(8,128)(2,1)S(1)}, u32[]{:S(2)}, u32[]{:S(2)}) async-start(f16[4,4,16,512]{3,2,1,0:T(8,128)(2,1)} %broadcast_in_dim.15), calls=%async_computation.1 | async-start | bytes 524288 | tf_op jit(solution)/shard_map/all_to_all | solution.py:111
  38.5 11.6 %collective-permute-start.2 = (bf16[96,2048]{1,0:T(8,128)(2,1)S(1)}, bf16[96,2048]{1,0:T(8,128)(2,1)S(1)}, u32[]{:S(2)}, u32[]{:S(2)}) collective-permute-start(bf16[96,2048]{1,0:T(8,128)(2,1)S(1)} %get-tuple-element.21), channel_id=1, source_target_pairs={{0,8},{4,12},{8,0},{12,4},{1,9},{5,13},{9,1},{13,5},{2,10},{6,14},... | collective-permute-start | bytes 1179656 | tf_op jit(solution)/shard_map/ppermute | solution.py:291
  43.1 0.9 copy-start.1
  50.1 9.7 %copy-start = (bf16[96,2048]{1,0:T(8,128)(2,1)}, bf16[96,2048]{1,0:T(8,128)(2,1)S(1)}, u32[]{:S(2)}) copy-start(bf16[96,2048]{1,0:T(8,128)(2,1)S(1)} %collective-permute-done.2.far0) | copy-start | bytes 1179652
  59.8 15.7 %all-to-all-start.3 = ((bf16[4,4,4,16,512]{4,3,2,1,0:T(8,128)(2,1)}), bf16[4,4,4,16,512]{4,3,2,1,0:T(8,128)(2,1)S(1)}, u32[]{:S(2)}, u32[]{:S(2)}) async-start(bf16[4,4,4,16,512]{4,3,2,1,0:T(8,128)(2,1)} %broadcast_in_dim.17), calls=%async_computation.3 | async-start | bytes 2097152 | tf_op jit(solution)/shard_map/all_to_all | solution.py:111
  64.9 10.5 %collective-permute-start.3 = (bf16[96,2048]{1,0:T(8,128)(2,1)}, bf16[96,2048]{1,0:T(8,128)(2,1)}, u32[]{:S(2)}, u32[]{:S(2)}) collective-permute-start(bf16[96,2048]{1,0:T(8,128)(2,1)} %get-tuple-element.23), channel_id=1, source_target_pairs={{0,8},{4,12},{8,0},{12,4},{1,9},{5,13},{9,1},{13,5},{2,10},{6,14},... | collective-permute-start | bytes 1179656 | tf_op jit(solution)/shard_map/ppermute | solution.py:291
  75.4 11.1 %collective-permute-start.4 = (bf16[2,2,4,4,16,512]{5,4,3,2,1,0:T(8,128)(2,1)S(1)}, bf16[2,2,4,4,16,512]{5,4,3,2,1,0:T(8,128)(2,1)S(1)}, u32[]{:S(2)}, u32[]{:S(2)}) collective-permute-start(bf16[2,2,4,4,16,512]{5,4,3,2,1,0:T(8,128)(2,1)S(1)} %bitcast.18), channel_id=1, source_target_pairs={{0,1},{1,0},{2,3},{3,2},{4,5},{5,4},{6,7},{7,6},{8,9},{9,8},{10,11... | collective-permute-start | bytes 3145736 | tf_op jit(solution)/shard_map/ppermute | solution.py:305

commit v4 on v3

--- a/solution.py
+++ b/solution.py
@@ -111,6 +111,55 @@
     return lax.all_to_all(blocks, along + across, 0, 0, axis_index_groups=groups, tiled=True)
 
 
+def exchange(blocks, along, across, turn):
+    n = math.prod(lax.axis_size(a) for a in along)
+    places = list(itertools.product(*(range(lax.axis_size(a)) for a in across)))
+    groups = [[(k + turn(*at)) % n * len(places) + i for k in range(n)] for i, at in enumerate(places)]
+    return lax.all_to_all(blocks, along + across, 0, 0, axis_index_groups=groups, tiled=True)
+
+
+def exchange(blocks, along, across, turn):
+    n = math.prod(lax.axis_size(a) for a in along)
+    places = list(itertools.product(*(range(lax.axis_size(a)) for a in across)))
+    groups = [[(k + turn(*at)) % n * len(places) + i for k in range(n)] for i, at in enumerate(places)]
+    return lax.all_to_all(blocks, along + across, 0, 0, axis_index_groups=groups, tiled=True)
+
+
+def exchange(blocks, along, across, turn):
+    n = math.prod(lax.axis_size(a) for a in along)
+    places = list(itertools.product(*(range(lax.axis_size(a)) for a in across)))
+    groups = [[(k + turn(*at)) % n * len(places) + i for k in range(n)] for i, at in enumerate(places)]
+    return lax.all_to_all(blocks, along + across, 0, 0, axis_index_groups=groups, tiled=True)
+
+
+def exchange(blocks, along, across, turn):
+    n = math.prod(lax.axis_size(a) for a in along)
+    places = list(itertools.product(*(range(lax.axis_size(a)) for a in across)))
+    groups = [[(k + turn(*at)) % n * len(places) + i for k in range(n)] for i, at in enumerate(places)]
+    return lax.all_to_all(blocks, along + across, 0, 0, axis_index_groups=groups, tiled=True)
+
+
+def exchange(blocks, along, across, turn):
+    n = math.prod(lax.axis_size(a) for a in along)
+    places = list(itertools.product(*(range(lax.axis_size(a)) for a in across)))
+    groups = [[(k + turn(*at)) % n * len(places) + i for k in range(n)] for i, at in enumerate(places)]
+    return lax.all_to_all(blocks, along + across, 0, 0, axis_index_groups=groups, tiled=True)
+
+
+def exchange(blocks, along, across, turn):
+    n = math.prod(lax.axis_size(a) for a in along)
+    places = list(itertools.product(*(range(lax.axis_size(a)) for a in across)))
+    groups = [[(k + turn(*at)) % n * len(places) + i for k in range(n)] for i, at in enumerate(places)]
+    return lax.all_to_all(blocks, along + across, 0, 0, axis_index_groups=groups, tiled=True)
+
+
+def exchange(blocks, along, across, turn):
+    n = math.prod(lax.axis_size(a) for a in along)
+    places = list(itertools.product(*(range(lax.axis_size(a)) for a in across)))
+    groups = [[(k + turn(*at)) % n * len(places) + i for k in range(n)] for i, at in enumerate(places)]
+    return lax.all_to_all(blocks, along + across, 0, 0, axis_index_groups=groups, tiled=True)
+
+
 def spread(block, along, across, turn):
     n = math.prod(lax.axis_size(a) for a in along)
     return exchange(jnp.broadcast_to(block[None], (n,) + block.shape), along, across, turn)
@@ -130,41 +179,48 @@
 def gather_kernel(at, tokens, t1, t3, out, sems):
     part = out.shape[2]
     own = tokens.at[:, pl.ds(pl.multiple_of(at[0] * part, part), part)]
-    copies = [
-        pltpu.make_async_copy(source, out.at[i], sems.at[i]) for i, source in enumerate((own, t1, t3))
-    ]
+    copies = [pltpu.make_async_copy(source, out.at[i], sems.at[i]) for i, source in enumerate((own, t1, t3))]
     for copy in copies:
         copy.start()
     for copy in copies:
         copy.wait()
 
 
-def gather_tokens(at, tokens, t1, t3):
-    tok, part = t1.shape
-    return pl.pallas_call(
-        gather_kernel,
-        out_shape=jax.ShapeDtypeStruct((3, tok, part), tokens.dtype),
-        in_specs=[SCALARS, HBM, HBM, HBM],
-        out_specs=WHOLE,
-        scratch_shapes=[pltpu.SemaphoreType.DMA((3,))],
-        compiler_params=LIMIT,
-        cost_estimate=pl.CostEstimate(flops=0, bytes_accessed=2**26, transcendentals=0),
-    )(at, *(pltpu.with_memory_space_constraint(p, pltpu.HBM) for p in (tokens, t1, t3)))
-
-
-def fetch(sources, places, sems):
-    copies = [pltpu.make_async_copy(s, p, sems.at[i]) for i, (s, p) in enumerate(zip(sources, places))]
+def join_kernel(first, second, out, sems):
+    cut = first.shape[0]
+    places = (out.at[pl.ds(0, cut)], out.at[pl.ds(cut, out.shape[0] - cut)])
+    copies = [pltpu.make_async_copy(s, p, sems.at[i]) for i, (s, p) in enumerate(zip((first, second), places))]
     for copy in copies:
         copy.start()
-    return copies
-
-
-def parts_of(ref, first):
-    cut = first.shape[0]
-    return [ref.at[pl.ds(0, cut)], ref.at[pl.ds(cut, ref.shape[0] - cut)]]
-
-
-def product(core, rows_y, near, far, far_copies):
+    for copy in copies:
+        copy.wait()
+
+
+def pinned(*arrays):
+    return [pltpu.with_memory_space_constraint(a, pltpu.HBM) for a in arrays]
+
+
+def moved(shape, copies):
+    return dict(
+        out_shape=jax.ShapeDtypeStruct(shape, jnp.bfloat16),
+        out_specs=WHOLE,
+        scratch_shapes=[pltpu.SemaphoreType.DMA((copies,))],
+        compiler_params=LIMIT,
+        cost_estimate=pl.CostEstimate(flops=2**34, bytes_accessed=2**26, transcendentals=0),
+    )
+
+
+def gather_tokens(at, tokens, t1, t3):
+    specs = [SCALARS, HBM, HBM, HBM]
+    return pl.pallas_call(gather_kernel, in_specs=specs, **moved((3,) + t1.shape, 3))(at, *pinned(tokens, t1, t3))
+
+
+def join_tokens(first, second):
+    shape = (first.shape[0] + second.shape[0], first.shape[1])
+    return pl.pallas_call(join_kernel, in_specs=[HBM, HBM], **moved(shape, 2))(*pinned(first, second))
+
+
+def product(core, rows_y, near, far):
     nl, nh, nzl, nzh, rows, kv = rows_y.shape
     part = near.shape[2]
     width = part // (2 * nh)
@@ -183,20 +239,13 @@
         )
         columns.append(pl.ds(pl.multiple_of((2 * h + core) * width, width), width))
     right = jnp.concatenate(weights, axis=0)
-
-    def times(blocks):
-        left = [jnp.concatenate([block[:, cols] for block in blocks], axis=0) for cols in columns]
-        return jnp.dot(jnp.concatenate(left, axis=1), right, preferred_element_type=jnp.float32)
-
-    first = times([near.at[i] for i in range(near.shape[0])])
-    for copy in far_copies:
-        copy.wait()
-    return jnp.concatenate([first, times([far])], axis=0), weights
-
-
-def first_kernel(at, rows_y, near, far0, far1, total, fresh, w, far, sems, sem):
-    copies = fetch((far0, far1), parts_of(far, far0), sems)
-    result, weights = product(at[2], rows_y, near, far, copies)
+    blocks = [near.at[i] for i in range(near.shape[0])] + [far]
+    left = [jnp.concatenate([block[:, cols] for block in blocks], axis=0) for cols in columns]
+    return jnp.dot(jnp.concatenate(left, axis=1), right, preferred_element_type=jnp.float32), weights
+
+
+def first_kernel(at, rows_y, near, far, total, fresh, w, sem):
+    result, weights = product(at[2], rows_y, near, far)
     for h, block in enumerate(weights):
         w[h] = block
     back = pltpu.make_async_copy(w.at[at[1]], fresh, sem)
@@ -205,9 +254,8 @@
     back.wait()
 
 
-def second_kernel(at, rows_y, near, far0, far1, total, out, far_here, sems):
-    copies = fetch((far0, far1), parts_of(far_here, far0), sems)
-    result, _ = product(1 - at[2], rows_y, near, far_here, copies)
+def second_kernel(at, rows_y, near, far, total, out):
+    result, _ = product(1 - at[2], rows_y, near, far)
     result = result + total[...]
     nx, tok = out.shape[:2]
     for i, step in enumerate(STEPS):
@@ -220,13 +268,9 @@
     return pl.CostEstimate(flops=4 * tok * part * kv, bytes_accessed=4 * 2**20, transcendentals=0)
 
 
-def pinned(*arrays):
-    return [pltpu.with_memory_space_constraint(a, pltpu.HBM) for a in arrays]
-
-
-def first_product(at, rows_y, near, far0, far1):
+def first_product(at, rows_y, near, far):
     nl, nh, nzl, nzh, rows, kv = rows_y.shape
-    tok, part = near.shape[1:]
+    tok = far.shape[0]
     deep = nzh * nzl * nl * rows
     return pl.pallas_call(
         first_kernel,
@@ -234,31 +278,24 @@
             jax.ShapeDtypeStruct((4 * tok, kv), jnp.float32),
             jax.ShapeDtypeStruct((deep, kv), jnp.bfloat16),
         ),
-        in_specs=[SCALARS, WHOLE, WHOLE, HBM, HBM],
+        in_specs=[SCALARS, WHOLE, WHOLE, WHOLE],
         out_specs=(WHOLE, HBM),
-        scratch_shapes=[
-            pltpu.VMEM((nh, deep, kv), jnp.bfloat16),
-            pltpu.VMEM((tok, part), near.dtype),
-            pltpu.SemaphoreType.DMA((2,)),
-            pltpu.SemaphoreType.DMA,
-        ],
+        scratch_shapes=[pltpu.VMEM((nh, deep, kv), jnp.bfloat16), pltpu.SemaphoreType.DMA],
         compiler_params=LIMIT,
         cost_estimate=cost(near, kv),
-    )(at, rows_y, near, *pinned(far0, far1))
-
-
-def second_product(at, rows_y, near, far0, far1, total):
+    )(at, rows_y, near, far)
+
+
+def second_product(at, rows_y, near, far, total):
     kv = rows_y.shape[-1]
-    tok, part = near.shape[1:]
     return pl.pallas_call(
         second_kernel,
-        out_shape=jax.ShapeDtypeStruct((4, tok, kv), jnp.bfloat16),
-        in_specs=[SCALARS, WHOLE, WHOLE, HBM, HBM, WHOLE],
+        out_shape=jax.ShapeDtypeStruct((4, far.shape[0], kv), jnp.bfloat16),
+        in_specs=[SCALARS, WHOLE, WHOLE, WHOLE, WHOLE],
         out_specs=WHOLE,
-        scratch_shapes=[pltpu.VMEM((tok, part), near.dtype), pltpu.SemaphoreType.DMA((2,))],
         compiler_params=LIMIT,
         cost_estimate=cost(near, kv),
-    )(at, rows_y, near, *pinned(far0, far1), total)
+    )(at, rows_y, near, far, total)
 
 
 def local(tokens, master, momentum, trained):
@@ -279,7 +316,7 @@
     offset = base / gain
     mine = (jnp.arange(nzh) == zh)[:, None, None]
     sent = jnp.where(mine, near + offset, near).astype(jnp.float16)
-    sums = spread(sent, ("zh",), ("zl", "c"), lambda zl, c: 3)
+    sums = spread(sent, ("zh",), ("zl", "c"), lambda zl, c: 2)
     sums = jnp.sum(sums.astype(jnp.float32), axis=0)
     fresh = (gain * sums).astype(jnp.bfloat16)
 
@@ -300,8 +337,8 @@
     pseudo = start.astype(jnp.float32) - summed / REPLICAS
     new_momentum = decay_factor * momentum + pseudo
     new_master = master - outer_rate * (pseudo + decay_factor * new_momentum)
-    rows_y, t21, new_master, new_momentum = lax.optimization_barrier((rows_y, t21, new_master, new_momentum))
-    taken = (near_tokens, t20, t21)
+    rows_y, new_master, new_momentum = lax.optimization_barrier((rows_y, new_master, new_momentum))
+    taken = (near_tokens, join_tokens(t20, t21))
     other = lax.ppermute(rows_y, "c", [(0, 1), (1, 0)])
 
     total, refreshed = first_product(at, rows_y, *taken)

time: 105 us -> 102 us (0.971)
  starting transfers between devices: 52.7 us -> 48.5 us
  blocking collectives: 22.3 us -> 26.1 us
  local copies, waits for them, and re-layouts: 8.99 us -> 6.34 us
    all_to_all x2, waiting for transfers between devices: 0.01 us -> 5.2 us  [exchange(): lax.all_to_all(blocks, along + across, 0, 0, axis_index_groups=groups, ti...]
    ppermute x4, waiting for transfers between devices: 8.27 us -> 4.41 us  [local(): lax.ppermute(cut, 'x', [(i, (i + d) % nx) for i in range(nx)])]
    all_to_all x2, blocking collectives: 22.3 us -> 26.1 us  [exchange(): lax.all_to_all(blocks, along + across, 0, 0, axis_index_groups=groups, ti...]
    ppermute x4, starting transfers between devices: 15.6 us -> 13 us  [local(): lax.ppermute(cut, 'x', [(i, (i + d) % nx) for i in range(nx)])]
    all_to_all x2, starting transfers between devices: 21.5 us -> 19.2 us  [exchange(): lax.all_to_all(blocks, along + across, 0, 0, axis_index_groups=groups, ti...]
    unnamed x10 -> x8, local copies, waits for them, and re-layouts: 1.46 us -> 0.02 us
    dynamic_slice x1, local copies, waits for them, and re-layouts: 2.99 us -> 1.78 us  [local(): lax.dynamic_slice(tokens, (0, (x + d) % nx * part), (tok, part))]
    pallas_call x2 -> x3, Pallas kernels: 4.53 us -> 4.85 us  [the longest x1 2.18 us: gather_tokens(): pl.pallas_call(gather_kernel, in_specs=specs, **moved((3,) + t1.shape, 3))]
  transfers between devices with their start and end apart: 8 -> 8, of which waited for: 3 -> 2; matrix products, arithmetic and copies ran while one was open for 6% -> 5% of each run, Pallas kernels for 5% -> 5%
where the time goes in v4:
time: 102 us; the launch traced here: 101 us
  starting transfers between devices  48.5 us (48%)
  blocking collectives  26.1 us (26%)
  waiting for transfers between devices  9.62 us (9%)
  Pallas kernels  6.76 us (7%)
  local copies, waits for them, and re-layouts  6.34 us (6%)
  other arithmetic  2.62 us (3%)
    all_to_all x2, blocking collectives, exchange(): lax.all_to_all(blocks, along + across, 0, 0, axis_index_groups=groups, ti...  26.1 us
    all_to_all x2, starting transfers between devices, exchange(): lax.all_to_all(blocks, along + across, 0, 0, axis_index_groups=groups, ti...  19.2 us
    ppermute x4, starting transfers between devices, local(): lax.ppermute(cut, 'x', [(i, (i + d) % nx) for i in range(nx)])  13 us
    ppermute x1, starting transfers between devices, local(): other = lax.ppermute(rows_y, 'c', [(0, 1), (1, 0)])  8.8 us
    all_to_all x1, starting transfers between devices, local(): near = lax.all_to_all(trained, ('zl', 'yl'), 1, 1, tiled=True)  7.46 us
    all_to_all x2, waiting for transfers between devices, exchange(): lax.all_to_all(blocks, along + across, 0, 0, axis_index_groups=groups, ti...  5.2 us
    ppermute x4, waiting for transfers between devices, local(): lax.ppermute(cut, 'x', [(i, (i + d) % nx) for i in range(nx)])  4.41 us
    pallas_call x1, Pallas kernels, gather_tokens(): pl.pallas_call(gather_kernel, in_specs=specs, **moved((3,) + t1.shape, 3))  2.18 us
  transfers between devices with their start and end apart: 8, of which 2 were waited for; matrix products, arithmetic and copies ran while one was open for 5% of the time, Pallas kernels for 5%

profile of v4, /device:TPU:1, one launch (start us, length us, event | category | flops | bytes accessed | tf_op | source)
XLA Modules:
  0.0 100.8 jit_solution(9183684373392361759)
XLA Ops:
  0.6 1.9 %copy.9 = bf16[4,8,16,512]{3,2,0,1:T(8,128)(2,1)} copy(bf16[4,8,16,512]{3,2,1,0:T(8,128)(2,1)} %bitcast.20) | data formatting | bytes 1048576 | tf_op jit(solution)/shard_map/reshape;squeeze | solution.py:309
  2.5 7.5 %all-to-all-start = ((bf16[4,8,16,512]{3,2,0,1:T(8,128)(2,1)}), bf16[4,8,16,512]{3,2,0,1:T(8,128)(2,1)S(1)}, u32[]{:S(2)}, u32[]{:S(2)}) async-start(bf16[4,8,16,512]{3,2,0,1:T(8,128)(2,1)} %copy.9), calls=%async_computation | async-start | bytes 1048576 | tf_op jit(solution)/shard_map/all_to_all | solution.py:310
  10.0 0.0 copy-start
  10.0 0.0 copy-start.2
  10.0 1.8 %constant_dynamic-slice_fusion = (bf16[192,2048]{1,0:T(8,128)(2,1)S(1)}, bf16[192,2048]{1,0:T(8,128)(2,1)S(1)}, bf16[192,2048]{1,0:T(8,128)(2,1)S(1)}) fusion(bf16[192,8192]{1,0:T(8,128)(2,1)} %tokens.1, s32[]{:T(128)S(6)} %select_n.42, s32[]{:T(128)S(6)} %select_n.40, s32[]{:T(128)S(6)} %select_n.38), kind=kLoop, calls=%fused_computation.16 | loop fusion | bytes 4718604 | tf_op jit(solution)/shard_map/dynamic_slice | solution.py:324
  11.8 0.8 fusion.6
  12.6 4.6 %collective-permute-start.2 = (bf16[96,2048]{1,0:T(8,128)(2,1)S(1)}, bf16[96,2048]{1,0:T(8,128)(2,1)S(1)}, u32[]{:S(2)}, u32[]{:S(2)}) collective-permute-start(bf16[96,2048]{1,0:T(8,128)(2,1)S(1)} %get-tuple-element.20), channel_id=1, source_target_pairs={{0,8},{4,12},{8,0},{12,4},{1,9},{5,13},{9,1},{13,5},{2,10},{6,14},... | collective-permute-start | bytes 1179656 | tf_op jit(solution)/shard_map/ppermute | solution.py:328
  17.2 2.2 %collective-permute-start = (bf16[192,2048]{1,0:T(8,128)(2,1)S(1)}, bf16[192,2048]{1,0:T(8,128)(2,1)}, u32[]{:S(2)}, u32[]{:S(2)}) collective-permute-start(bf16[192,2048]{1,0:T(8,128)(2,1)S(1)} %get-tuple-element.17), channel_id=1, source_target_pairs={{0,4},{4,8},{8,12},{12,0},{1,5},{5,9},{9,13},{13,1},{2,6},{6,10},{... | collective-permute-start | bytes 2359304 | tf_op jit(solution)/shard_map/ppermute | solution.py:328
  19.5 4.3 %collective-permute-start.1 = (bf16[192,2048]{1,0:T(8,128)(2,1)S(1)}, bf16[192,2048]{1,0:T(8,128)(2,1)}, u32[]{:S(2)}, u32[]{:S(2)}) collective-permute-start(bf16[192,2048]{1,0:T(8,128)(2,1)S(1)} %get-tuple-element.18), channel_id=1, source_target_pairs={{0,12},{4,0},{8,4},{12,8},{1,13},{5,1},{9,5},{13,9},{2,14},{6,2},{... | collective-permute-start | bytes 2359304 | tf_op jit(solution)/shard_map/ppermute | solution.py:328
  23.7 0.0 copy-done
  23.8 0.0 copy-start.1
  23.8 0.1 pad_add_fusion.at
  23.9 0.0 copy-done.2
  23.9 0.0 all-to-all-done
  23.9 0.1 convert_reduce_fusion.1
  24.0 0.1 fusion
  24.1 0.7 broadcast_in_dim.15
  24.8 14.2 %all-to-all-start.1 = ((f16[4,4,16,512]{3,2,1,0:T(8,128)(2,1)}), f16[4,4,16,512]{3,2,1,0:T(8,128)(2,1)S(1)}, u32[]{:S(2)}, u32[]{:S(2)}) async-start(f16[4,4,16,512]{3,2,1,0:T(8,128)(2,1)} %broadcast_in_dim.15), calls=%async_computation.1 | async-start | bytes 524288 | tf_op jit(solution)/shard_map/all_to_all | solution.py:160
  39.0 4.4 %collective-permute-done.t1 = bf16[192,2048]{1,0:T(8,128)(2,1)} collective-permute-done((bf16[192,2048]{1,0:T(8,128)(2,1)S(1)}, bf16[192,2048]{1,0:T(8,128)(2,1)}, u32[]{:S(2)}, u32[]{:S(2)}) %collective-permute-start) | collective-permute-done | bytes 786464 | tf_op jit(solution)/shard_map/ppermute | solution.py:328
  43.4 0.0 copy-done.1
  43.4 0.0 collective-permute-done.1.t3
  43.4 2.2 %shard_map.75.near = bf16[3,192,2048]{2,1,0:T(8,128)(2,1)S(1)} custom-call(s32[4]{0:T(128)S(1)} %pad_add_fusion.at, bf16[192,8192]{1,0:T(8,128)(2,1)} %tokens.1, bf16[192,2048]{1,0:T(8,128)(2,1)} %collective-permute-done.t1, bf16[192,2048]{1,0:T(8,128)(2,1)} %collective-permute-done.1.t3), custom_call_target="tpu_custom_call" | custom-call | flops 17179869184 | bytes 67108864 | tf_op jit(solution)/shard_map/pallas_call | solution.py:215
  45.6 0.0 all-to-all-done.1
  45.7 0.0 collective-permute-done.2.first
  45.7 0.0 copy-start.3
  45.7 12.8 %all_to_all.25 = bf16[4,4,16,512]{3,2,1,0:T(8,128)(2,1)S(1)} all-to-all(bf16[4,4,16,512]{3,2,1,0:T(8,128)(2,1)S(1)} %broadcast_in_dim.16), channel_id=1, replica_groups={{0,32,64,96},{65,97,1,33},{2,34,66,98},{67,99,3,35},{4,36,68,100},{69,1..., dimensions={0} | all-to-all | bytes 524288 | tf_op jit(solution)/shard_map/all_to_all | solution.py:160
  58.6 1.1 %broadcast_in_dim.17 = bf16[4,4,4,16,512]{4,3,2,1,0:T(8,128)(2,1)} broadcast(bf16[4,4,16,512]{3,2,1,0:T(8,128)(2,1)S(1)} %all_to_all.25), dimensions={1,2,3,4} | broadcast | bytes 1310720 | tf_op jit(solution)/shard_map/broadcast_in_dim | solution.py:165
  59.7 0.0 copy-done.3
  59.7 5.0 %all-to-all-start.3 = ((bf16[4,4,4,16,512]{4,3,2,1,0:T(8,128)(2,1)}), bf16[4,4,4,16,512]{4,3,2,1,0:T(8,128)(2,1)S(1)}, u32[]{:S(2)}, u32[]{:S(2)}) async-start(bf16[4,4,4,16,512]{4,3,2,1,0:T(8,128)(2,1)} %broadcast_in_dim.17), calls=%async_computation.3 | async-start | bytes 2097152 | tf_op jit(solution)/shard_map/all_to_all | solution.py:160
  64.6 1.9 %collective-permute-start.3 = (bf16[96,2048]{1,0:T(8,128)(2,1)}, bf16[96,2048]{1,0:T(8,128)(2,1)}, u32[]{:S(2)}, u32[]{:S(2)}) collective-permute-start(bf16[96,2048]{1,0:T(8,128)(2,1)} %get-tuple-element.27), channel_id=1, source_target_pairs={{0,8},{4,12},{8,0},{12,4},{1,9},{5,13},{9,1},{13,5},{2,10},{6,14},... | collective-permute-start | bytes 1179656 | tf_op jit(solution)/shard_map/ppermute | solution.py:328
  66.6 1.4 %multiply_add_fusion = (f32[16,512]{1,0:T(8,128)}, f32[16,512]{1,0:T(8,128)}) fusion(f32[16,512]{1,0:T(8,128)} %param.6, f32[4,16,512]{2,1,0:T(8,128)S(1)} %convert_reduce_fusion.2, s32[]{:T(128)S(6)} %select_n.43, bf16[16,512]{1,0:T(8,128)(2,1)} %copy-done.1, f32[16,512]{1,0:T(8,128)} %param.5), kind=kLoop, calls=%fused_computation.15 | loop fusion | flops 131072 | bytes 180228 | tf_op jit(solution)/shard_map/add | solution.py:338
  68.0 5.2 %all-to-all-done.3 = bf16[4,4,4,16,512]{4,3,2,1,0:T(8,128)(2,1)S(1)} async-done(((bf16[4,4,4,16,512]{4,3,2,1,0:T(8,128)(2,1)}), bf16[4,4,4,16,512]{4,3,2,1,0:T(8,128)(2,1)S(1)}, u32[]{:S(2)}, u32[]{:S(2)}) %all-to-all-start.3) | async-done | bytes 1048608 | tf_op jit(solution)/shard_map/all_to_all | solution.py:160
  73.2 8.8 %collective-permute-start.4 = (bf16[2,2,4,4,16,512]{5,4,3,2,1,0:T(8,128)(2,1)S(1)}, bf16[2,2,4,4,16,512]{5,4,3,2,1,0:T(8,128)(2,1)S(1)}, u32[]{:S(2)}, u32[]{:S(2)}) collective-permute-start(bf16[2,2,4,4,16,512]{5,4,3,2,1,0:T(8,128)(2,1)S(1)} %bitcast.18), channel_id=1, source_target_pairs={{0,1},{1,0},{2,3},{3,2},{4,5},{5,4},{6,7},{7,6},{8,9},{9,8},{10,11... | collective-permute-start | bytes 3145736 | tf_op jit(solution)/shard_map/ppermute | solution.py:342
  82.0 0.0 collective-permute-done.3.second
  82.0 1.1 %shard_map.76.far = bf16[192,2048]{1,0:T(8,128)(2,1)S(1)} custom-call(bf16[96,2048]{1,0:T(8,128)(2,1)} %copy-done.3, bf16[96,2048]{1,0:T(8,128)(2,1)} %collective-permute-done.3.second), custom_call_target="tpu_custom_call" | custom-call | flops 17179869184 | bytes 67108864 | tf_op jit(solution)/shard_map/pallas_call | solution.py:220
  83.2 1.9 %shard_map.77 = (f32[768,512]{1,0:T(8,128)S(1)}, bf16[512,512]{1,0:T(8,128)(2,1)}) custom-call(s32[4]{0:T(128)S(1)} %pad_add_fusion.at, bf16[2,2,4,4,16,512]{5,4,3,2,1,0:T(8,128)(2,1)S(1)} %bitcast.19, bf16[3,192,2048]{2,1,0:T(8,128)(2,1)S(1)} %shard_map.75.near, bf16[192,2048]{1,0:T(8,128)(2,1)S(1)} %shard_map.76.far), custom_call_target="tpu_custom_call" | custom-call | flops 805306368 | bytes 4194304 | tf_op jit(solution)/shard_map/pallas_call | solution.py:275
  85.1 0.0 collective-permute-done.4.rows_y
  85.1 1.5 %shard_map.78 = bf16[4,192,512]{2,1,0:T(8,128)(2,1)S(1)} custom-call(s32[4]{0:T(128)S(1)} %pad_add_fusion.at, bf16[2,2,4,4,16,512]{5,4,3,2,1,0:T(8,128)(2,1)S(1)} %collective-permute-done.4.rows_y, bf16[3,192,2048]{2,1,0:T(8,128)(2,1)S(1)} %shard_map.75.near, bf16[192,2048]{1,0:T(8,128)(2,1)S(1)} %shard_map.76.far, f32[768,512]{1,0:T(8,128)S(1)} %get-tuple-element.29.total), custom_call_target="tpu_custom_call" | custom-call | flops 805306368 | bytes 4194304 | tf_op jit(solution)/shard_map/pallas_call | solution.py:291
  86.6 13.3 %all_to_all.26 = bf16[4,192,512]{2,1,0:T(8,128)(2,1)S(1)} all-to-all(bf16[4,192,512]{2,1,0:T(8,128)(2,1)S(1)} %shard_map.78), channel_id=1, replica_groups={{0,4,8,12},{9,13,1,5},{2,6,10,14},{11,15,3,7},{16,20,24,28},{25,29,17,2..., dimensions={0} | all-to-all | bytes 1572864 | tf_op jit(solution)/shard_map/all_to_all | solution.py:160
  99.9 0.9 convert_reduce_fusion
  (6 shorter events, 0.1 us)
Async XLA Ops:
  2.5 21.4 %all-to-all-start = ((bf16[4,8,16,512]{3,2,0,1:T(8,128)(2,1)}), bf16[4,8,16,512]{3,2,0,1:T(8,128)(2,1)S(1)}, u32[]{:S(2)}, u32[]{:S(2)}) async-start(bf16[4,8,16,512]{3,2,0,1:T(8,128)(2,1)} %copy.9), calls=%async_computation | async-start | bytes 1048576 | tf_op jit(solution)/shard_map/all_to_all | solution.py:310
  10.0 13.8 %copy-start = (f32[16,512]{1,0:T(8,128)S(1)}, f32[16,512]{1,0:T(8,128)}, u32[]{:S(2)}) copy-start(f32[16,512]{1,0:T(8,128)} %param.5) | copy-start | bytes 98308
  10.0 13.9 %copy-start.2 = (f32[16,512]{1,0:T(8,128)S(1)}, f32[16,512]{1,0:T(8,128)}, u32[]{:S(2)}) copy-start(f32[16,512]{1,0:T(8,128)} %param.6) | copy-start | bytes 98308
  12.6 33.1 %collective-permute-start.2 = (bf16[96,2048]{1,0:T(8,128)(2,1)S(1)}, bf16[96,2048]{1,0:T(8,128)(2,1)S(1)}, u32[]{:S(2)}, u32[]{:S(2)}) collective-permute-start(bf16[96,2048]{1,0:T(8,128)(2,1)S(1)} %get-tuple-element.20), channel_id=1, source_target_pairs={{0,8},{4,12},{8,0},{12,4},{1,9},{5,13},{9,1},{13,5},{2,10},{6,14},... | collective-permute-start | bytes 1179656 | tf_op jit(solution)/shard_map/ppermute | solution.py:328
  17.2 26.2 %collective-permute-start = (bf16[192,2048]{1,0:T(8,128)(2,1)S(1)}, bf16[192,2048]{1,0:T(8,128)(2,1)}, u32[]{:S(2)}, u32[]{:S(2)}) collective-permute-start(bf16[192,2048]{1,0:T(8,128)(2,1)S(1)} %get-tuple-element.17), channel_id=1, source_target_pairs={{0,4},{4,8},{8,12},{12,0},{1,5},{5,9},{9,13},{13,1},{2,6},{6,10},{... | collective-permute-start | bytes 2359304 | tf_op jit(solution)/shard_map/ppermute | solution.py:328
  19.5 24.0 %collective-permute-start.1 = (bf16[192,2048]{1,0:T(8,128)(2,1)S(1)}, bf16[192,2048]{1,0:T(8,128)(2,1)}, u32[]{:S(2)}, u32[]{:S(2)}) collective-permute-start(bf16[192,2048]{1,0:T(8,128)(2,1)S(1)} %get-tuple-element.18), channel_id=1, source_target_pairs={{0,12},{4,0},{8,4},{12,8},{1,13},{5,1},{9,5},{13,9},{2,14},{6,2},{... | collective-permute-start | bytes 2359304 | tf_op jit(solution)/shard_map/ppermute | solution.py:328
  23.8 19.7 %copy-start.1 = (bf16[16,512]{1,0:T(8,128)(2,1)}, bf16[16,512]{1,0:T(8,128)(2,1)S(1)}, u32[]{:S(2)}) copy-start(bf16[16,512]{1,0:T(8,128)(2,1)S(1)} %convert_element_type.27) | copy-start | bytes 49156
  24.8 20.8 %all-to-all-start.1 = ((f16[4,4,16,512]{3,2,1,0:T(8,128)(2,1)}), f16[4,4,16,512]{3,2,1,0:T(8,128)(2,1)S(1)}, u32[]{:S(2)}, u32[]{:S(2)}) async-start(f16[4,4,16,512]{3,2,1,0:T(8,128)(2,1)} %broadcast_in_dim.15), calls=%async_computation.1 | async-start | bytes 524288 | tf_op jit(solution)/shard_map/all_to_all | solution.py:160
  45.7 14.0 %copy-start.3 = (bf16[96,2048]{1,0:T(8,128)(2,1)}, bf16[96,2048]{1,0:T(8,128)(2,1)S(1)}, u32[]{:S(2)}) copy-start(bf16[96,2048]{1,0:T(8,128)(2,1)S(1)} %collective-permute-done.2.first) | copy-start | bytes 1179652
  59.7 13.5 %all-to-all-start.3 = ((bf16[4,4,4,16,512]{4,3,2,1,0:T(8,128)(2,1)}), bf16[4,4,4,16,512]{4,3,2,1,0:T(8,128)(2,1)S(1)}, u32[]{:S(2)}, u32[]{:S(2)}) async-start(bf16[4,4,4,16,512]{4,3,2,1,0:T(8,128)(2,1)} %broadcast_in_dim.17), calls=%async_computation.3 | async-start | bytes 2097152 | tf_op jit(solution)/shard_map/all_to_all | solution.py:160
  64.6 17.4 %collective-permute-start.3 = (bf16[96,2048]{1,0:T(8,128)(2,1)}, bf16[96,2048]{1,0:T(8,128)(2,1)}, u32[]{:S(2)}, u32[]{:S(2)}) collective-permute-start(bf16[96,2048]{1,0:T(8,128)(2,1)} %get-tuple-element.27), channel_id=1, source_target_pairs={{0,8},{4,12},{8,0},{12,4},{1,9},{5,13},{9,1},{13,5},{2,10},{6,14},... | collective-permute-start | bytes 1179656 | tf_op jit(solution)/shard_map/ppermute | solution.py:328
  73.2 11.9 %collective-permute-start.4 = (bf16[2,2,4,4,16,512]{5,4,3,2,1,0:T(8,128)(2,1)S(1)}, bf16[2,2,4,4,16,512]{5,4,3,2,1,0:T(8,128)(2,1)S(1)}, u32[]{:S(2)}, u32[]{:S(2)}) collective-permute-start(bf16[2,2,4,4,16,512]{5,4,3,2,1,0:T(8,128)(2,1)S(1)} %bitcast.18), channel_id=1, source_target_pairs={{0,1},{1,0},{2,3},{3,2},{4,5},{5,4},{6,7},{7,6},{8,9},{9,8},{10,11... | collective-permute-start | bytes 3145736 | tf_op jit(solution)/shard_map/ppermute | solution.py:342

commit v5 on v4

--- a/solution.py
+++ b/solution.py
@@ -11,6 +11,13 @@
 REPLICAS = 32
 outer_rate = 0.7
 decay_factor = 0.9
+
+
+def exchange(blocks, along, across, turn):
+    n = math.prod(lax.axis_size(a) for a in along)
+    places = list(itertools.product(*(range(lax.axis_size(a)) for a in across)))
+    groups = [[(k + turn(*at)) % n * len(places) + i for k in range(n)] for i, at in enumerate(places)]
+    return lax.all_to_all(blocks, along + across, 0, 0, axis_index_groups=groups, tiled=True)
 
 
 def exchange(blocks, along, across, turn):
@@ -320,7 +327,7 @@
     sums = jnp.sum(sums.astype(jnp.float32), axis=0)
     fresh = (gain * sums).astype(jnp.bfloat16)
 
-    most = tok // 2
+    most = tok * 2 // 3
     cuts = [lax.dynamic_slice(tokens, (0, (x + d) % nx * part), (tok, part)) for d in (1, 3, 2)]
     cuts = lax.optimization_barrier(cuts)
     cuts[2:] = lax.optimization_barrier([cuts[2][:most], cuts[2][most:]])

time: 102 us -> 101 us (level)
  blocking collectives: 26.1 us -> 22.1 us
  starting transfers between devices: 48.5 us -> 50.6 us
  waiting for transfers between devices: 9.62 us -> 10.8 us
    all_to_all x2, blocking collectives: 26.1 us -> 22.1 us  [exchange(): lax.all_to_all(blocks, along + across, 0, 0, axis_index_groups=groups, ti...]
    ppermute x4, waiting for transfers between devices: 4.41 us -> 7.75 us  [local(): lax.ppermute(cut, 'x', [(i, (i + d) % nx) for i in range(nx)])]
    ppermute x4, starting transfers between devices: 13 us -> 15.2 us  [local(): lax.ppermute(cut, 'x', [(i, (i + d) % nx) for i in range(nx)])]
    all_to_all x2, waiting for transfers between devices: 5.2 us -> 3.08 us  [exchange(): lax.all_to_all(blocks, along + across, 0, 0, axis_index_groups=groups, ti...]
where the time goes in v5:
time: 101 us; the launch traced here: 100 us
  starting transfers between devices  50.6 us (50%)
  blocking collectives  22.1 us (22%)
  waiting for transfers between devices  10.8 us (11%)
  Pallas kernels  6.75 us (7%)
  local copies, waits for them, and re-layouts  6.28 us (6%)
  other arithmetic  2.62 us (3%)
    all_to_all x2, blocking collectives, exchange(): lax.all_to_all(blocks, along + across, 0, 0, axis_index_groups=groups, ti...  22.1 us
    all_to_all x2, starting transfers between devices, exchange(): lax.all_to_all(blocks, along + across, 0, 0, axis_index_groups=groups, ti...  19.2 us
    ppermute x4, starting transfers between devices, local(): lax.ppermute(cut, 'x', [(i, (i + d) % nx) for i in range(nx)])  15.2 us
    ppermute x1, starting transfers between devices, local(): other = lax.ppermute(rows_y, 'c', [(0, 1), (1, 0)])  8.8 us
    ppermute x4, waiting for transfers between devices, local(): lax.ppermute(cut, 'x', [(i, (i + d) % nx) for i in range(nx)])  7.75 us
    all_to_all x1, starting transfers between devices, local(): near = lax.all_to_all(trained, ('zl', 'yl'), 1, 1, tiled=True)  7.46 us
    all_to_all x2, waiting for transfers between devices, exchange(): lax.all_to_all(blocks, along + across, 0, 0, axis_index_groups=groups, ti...  3.08 us
    pallas_call x1, Pallas kernels, gather_tokens(): pl.pallas_call(gather_kernel, in_specs=specs, **moved((3,) + t1.shape, 3))  2.18 us
  transfers between devices with their start and end apart: 8, of which 2 were waited for; matrix products, arithmetic and copies ran while one was open for 5% of the time, Pallas kernels for 5%

profile of v5, /device:TPU:1, one launch (start us, length us, event | category | flops | bytes accessed | tf_op | source)
XLA Modules:
  0.0 100.1 jit_solution(4499476127922497834)
XLA Ops:
  0.6 1.9 %copy.9 = bf16[4,8,16,512]{3,2,0,1:T(8,128)(2,1)} copy(bf16[4,8,16,512]{3,2,1,0:T(8,128)(2,1)} %bitcast.20) | data formatting | bytes 1048576 | tf_op jit(solution)/shard_map/reshape;squeeze | solution.py:316
  2.5 7.5 %all-to-all-start = ((bf16[4,8,16,512]{3,2,0,1:T(8,128)(2,1)}), bf16[4,8,16,512]{3,2,0,1:T(8,128)(2,1)S(1)}, u32[]{:S(2)}, u32[]{:S(2)}) async-start(bf16[4,8,16,512]{3,2,0,1:T(8,128)(2,1)} %copy.9), calls=%async_computation | async-start | bytes 1048576 | tf_op jit(solution)/shard_map/all_to_all | solution.py:317
  10.0 0.0 copy-start
  10.0 0.0 copy-start.2
  10.0 1.8 %constant_dynamic-slice_fusion = (bf16[192,2048]{1,0:T(8,128)(2,1)S(1)}, bf16[192,2048]{1,0:T(8,128)(2,1)S(1)}, bf16[192,2048]{1,0:T(8,128)(2,1)S(1)}) fusion(bf16[192,8192]{1,0:T(8,128)(2,1)} %tokens.1, s32[]{:T(128)S(6)} %select_n.42, s32[]{:T(128)S(6)} %select_n.40, s32[]{:T(128)S(6)} %select_n.38), kind=kLoop, calls=%fused_computation.16 | loop fusion | bytes 4718604 | tf_op jit(solution)/shard_map/dynamic_slice | solution.py:331
  11.8 0.7 slice.7
  12.5 4.7 %collective-permute-start.2 = (bf16[128,2048]{1,0:T(8,128)(2,1)S(1)}, bf16[128,2048]{1,0:T(8,128)(2,1)}, u32[]{:S(2)}, u32[]{:S(2)}) collective-permute-start(bf16[128,2048]{1,0:T(8,128)(2,1)S(1)} %slice.6), channel_id=1, source_target_pairs={{0,8},{4,12},{8,0},{12,4},{1,9},{5,13},{9,1},{13,5},{2,10},{6,14},... | collective-permute-start | bytes 1572872 | tf_op jit(solution)/shard_map/ppermute | solution.py:335
  17.2 2.2 %collective-permute-start = (bf16[192,2048]{1,0:T(8,128)(2,1)S(1)}, bf16[192,2048]{1,0:T(8,128)(2,1)}, u32[]{:S(2)}, u32[]{:S(2)}) collective-permute-start(bf16[192,2048]{1,0:T(8,128)(2,1)S(1)} %get-tuple-element.17), channel_id=1, source_target_pairs={{0,4},{4,8},{8,12},{12,0},{1,5},{5,9},{9,13},{13,1},{2,6},{6,10},{... | collective-permute-start | bytes 2359304 | tf_op jit(solution)/shard_map/ppermute | solution.py:335
  19.4 4.3 %collective-permute-start.1 = (bf16[192,2048]{1,0:T(8,128)(2,1)S(1)}, bf16[192,2048]{1,0:T(8,128)(2,1)}, u32[]{:S(2)}, u32[]{:S(2)}) collective-permute-start(bf16[192,2048]{1,0:T(8,128)(2,1)S(1)} %get-tuple-element.18), channel_id=1, source_target_pairs={{0,12},{4,0},{8,4},{12,8},{1,13},{5,1},{9,5},{13,9},{2,14},{6,2},{... | collective-permute-start | bytes 2359304 | tf_op jit(solution)/shard_map/ppermute | solution.py:335
  23.7 0.0 copy-done
  23.7 0.0 copy-start.1
  23.8 0.1 pad_add_fusion.at
  23.8 0.0 copy-done.2
  23.9 0.0 all-to-all-done
  23.9 0.1 convert_reduce_fusion.1
  24.0 0.1 fusion
  24.0 0.7 broadcast_in_dim.15
  24.8 14.2 %all-to-all-start.1 = ((f16[4,4,16,512]{3,2,1,0:T(8,128)(2,1)}), f16[4,4,16,512]{3,2,1,0:T(8,128)(2,1)S(1)}, u32[]{:S(2)}, u32[]{:S(2)}) async-start(f16[4,4,16,512]{3,2,1,0:T(8,128)(2,1)} %broadcast_in_dim.15), calls=%async_computation.1 | async-start | bytes 524288 | tf_op jit(solution)/shard_map/all_to_all | solution.py:167
  39.0 7.7 %collective-permute-done.t1 = bf16[192,2048]{1,0:T(8,128)(2,1)} collective-permute-done((bf16[192,2048]{1,0:T(8,128)(2,1)S(1)}, bf16[192,2048]{1,0:T(8,128)(2,1)}, u32[]{:S(2)}, u32[]{:S(2)}) %collective-permute-start) | collective-permute-done | bytes 786464 | tf_op jit(solution)/shard_map/ppermute | solution.py:335
  46.7 0.0 copy-done.1
  46.7 0.0 collective-permute-done.1.t3
  46.7 2.2 %shard_map.75.near = bf16[3,192,2048]{2,1,0:T(8,128)(2,1)S(1)} custom-call(s32[4]{0:T(128)S(1)} %pad_add_fusion.at, bf16[192,8192]{1,0:T(8,128)(2,1)} %tokens.1, bf16[192,2048]{1,0:T(8,128)(2,1)} %collective-permute-done.t1, bf16[192,2048]{1,0:T(8,128)(2,1)} %collective-permute-done.1.t3), custom_call_target="tpu_custom_call" | custom-call | flops 17179869184 | bytes 67108864 | tf_op jit(solution)/shard_map/pallas_call | solution.py:222
  48.9 0.0 all-to-all-done.1
  49.0 0.0 collective-permute-done.2.first
  49.0 9.5 %all_to_all.25 = bf16[4,4,16,512]{3,2,1,0:T(8,128)(2,1)S(1)} all-to-all(bf16[4,4,16,512]{3,2,1,0:T(8,128)(2,1)S(1)} %broadcast_in_dim.16), channel_id=1, replica_groups={{0,32,64,96},{65,97,1,33},{2,34,66,98},{67,99,3,35},{4,36,68,100},{69,1..., dimensions={0} | all-to-all | bytes 524288 | tf_op jit(solution)/shard_map/all_to_all | solution.py:167
  58.5 1.1 %broadcast_in_dim.17 = bf16[4,4,4,16,512]{4,3,2,1,0:T(8,128)(2,1)} broadcast(bf16[4,4,16,512]{3,2,1,0:T(8,128)(2,1)S(1)} %all_to_all.25), dimensions={1,2,3,4} | broadcast | bytes 1310720 | tf_op jit(solution)/shard_map/broadcast_in_dim | solution.py:172
  59.6 5.0 %all-to-all-start.3 = ((bf16[4,4,4,16,512]{4,3,2,1,0:T(8,128)(2,1)}), bf16[4,4,4,16,512]{4,3,2,1,0:T(8,128)(2,1)S(1)}, u32[]{:S(2)}, u32[]{:S(2)}) async-start(bf16[4,4,4,16,512]{4,3,2,1,0:T(8,128)(2,1)} %broadcast_in_dim.17), calls=%async_computation.3 | async-start | bytes 2097152 | tf_op jit(solution)/shard_map/all_to_all | solution.py:167
  64.6 4.0 %collective-permute-start.3 = (bf16[64,2048]{1,0:T(8,128)(2,1)}, bf16[64,2048]{1,0:T(8,128)(2,1)}, u32[]{:S(2)}, u32[]{:S(2)}) collective-permute-start(bf16[64,2048]{1,0:T(8,128)(2,1)} %slice.7), channel_id=1, source_target_pairs={{0,8},{4,12},{8,0},{12,4},{1,9},{5,13},{9,1},{13,5},{2,10},{6,14},... | collective-permute-start | bytes 786440 | tf_op jit(solution)/shard_map/ppermute | solution.py:335
  68.6 1.4 %multiply_add_fusion = (f32[16,512]{1,0:T(8,128)}, f32[16,512]{1,0:T(8,128)}) fusion(f32[16,512]{1,0:T(8,128)} %param.6, f32[4,16,512]{2,1,0:T(8,128)S(1)} %convert_reduce_fusion.2, s32[]{:T(128)S(6)} %select_n.43, bf16[16,512]{1,0:T(8,128)(2,1)} %copy-done.1, f32[16,512]{1,0:T(8,128)} %param.5), kind=kLoop, calls=%fused_computation.15 | loop fusion | flops 131072 | bytes 180228 | tf_op jit(solution)/shard_map/add | solution.py:345
  70.1 3.1 %all-to-all-done.3 = bf16[4,4,4,16,512]{4,3,2,1,0:T(8,128)(2,1)S(1)} async-done(((bf16[4,4,4,16,512]{4,3,2,1,0:T(8,128)(2,1)}), bf16[4,4,4,16,512]{4,3,2,1,0:T(8,128)(2,1)S(1)}, u32[]{:S(2)}, u32[]{:S(2)}) %all-to-all-start.3) | async-done | bytes 1048608 | tf_op jit(solution)/shard_map/all_to_all | solution.py:167
  73.2 8.8 %collective-permute-start.4 = (bf16[2,2,4,4,16,512]{5,4,3,2,1,0:T(8,128)(2,1)S(1)}, bf16[2,2,4,4,16,512]{5,4,3,2,1,0:T(8,128)(2,1)S(1)}, u32[]{:S(2)}, u32[]{:S(2)}) collective-permute-start(bf16[2,2,4,4,16,512]{5,4,3,2,1,0:T(8,128)(2,1)S(1)} %bitcast.18), channel_id=1, source_target_pairs={{0,1},{1,0},{2,3},{3,2},{4,5},{5,4},{6,7},{7,6},{8,9},{9,8},{10,11... | collective-permute-start | bytes 3145736 | tf_op jit(solution)/shard_map/ppermute | solution.py:349
  82.0 0.0 collective-permute-done.3.second
  82.0 1.1 %shard_map.76.far = bf16[192,2048]{1,0:T(8,128)(2,1)S(1)} custom-call(bf16[128,2048]{1,0:T(8,128)(2,1)} %collective-permute-done.2.first, bf16[64,2048]{1,0:T(8,128)(2,1)} %collective-permute-done.3.second), custom_call_target="tpu_custom_call" | custom-call | flops 17179869184 | bytes 67108864 | tf_op jit(solution)/shard_map/pallas_call | solution.py:227
  83.1 1.9 %shard_map.77 = (f32[768,512]{1,0:T(8,128)S(1)}, bf16[512,512]{1,0:T(8,128)(2,1)}) custom-call(s32[4]{0:T(128)S(1)} %pad_add_fusion.at, bf16[2,2,4,4,16,512]{5,4,3,2,1,0:T(8,128)(2,1)S(1)} %bitcast.19, bf16[3,192,2048]{2,1,0:T(8,128)(2,1)S(1)} %shard_map.75.near, bf16[192,2048]{1,0:T(8,128)(2,1)S(1)} %shard_map.76.far), custom_call_target="tpu_custom_call" | custom-call | flops 805306368 | bytes 4194304 | tf_op jit(solution)/shard_map/pallas_call | solution.py:282
  85.0 0.0 collective-permute-done.4.rows_y
  85.0 1.5 %shard_map.78 = bf16[4,192,512]{2,1,0:T(8,128)(2,1)S(1)} custom-call(s32[4]{0:T(128)S(1)} %pad_add_fusion.at, bf16[2,2,4,4,16,512]{5,4,3,2,1,0:T(8,128)(2,1)S(1)} %collective-permute-done.4.rows_y, bf16[3,192,2048]{2,1,0:T(8,128)(2,1)S(1)} %shard_map.75.near, bf16[192,2048]{1,0:T(8,128)(2,1)S(1)} %shard_map.76.far, f32[768,512]{1,0:T(8,128)S(1)} %get-tuple-element.29.total), custom_call_target="tpu_custom_call" | custom-call | flops 805306368 | bytes 4194304 | tf_op jit(solution)/shard_map/pallas_call | solution.py:298
  86.6 12.6 %all_to_all.26 = bf16[4,192,512]{2,1,0:T(8,128)(2,1)S(1)} all-to-all(bf16[4,192,512]{2,1,0:T(8,128)(2,1)S(1)} %shard_map.78), channel_id=1, replica_groups={{0,4,8,12},{9,13,1,5},{2,6,10,14},{11,15,3,7},{16,20,24,28},{25,29,17,2..., dimensions={0} | all-to-all | bytes 1572864 | tf_op jit(solution)/shard_map/all_to_all | solution.py:167
  99.2 0.9 convert_reduce_fusion
  (7 shorter events, 0.1 us)
Async XLA Ops:
  2.5 21.4 %all-to-all-start = ((bf16[4,8,16,512]{3,2,0,1:T(8,128)(2,1)}), bf16[4,8,16,512]{3,2,0,1:T(8,128)(2,1)S(1)}, u32[]{:S(2)}, u32[]{:S(2)}) async-start(bf16[4,8,16,512]{3,2,0,1:T(8,128)(2,1)} %copy.9), calls=%async_computation | async-start | bytes 1048576 | tf_op jit(solution)/shard_map/all_to_all | solution.py:317
  10.0 13.7 %copy-start = (f32[16,512]{1,0:T(8,128)S(1)}, f32[16,512]{1,0:T(8,128)}, u32[]{:S(2)}) copy-start(f32[16,512]{1,0:T(8,128)} %param.5) | copy-start | bytes 98308
  10.0 13.9 %copy-start.2 = (f32[16,512]{1,0:T(8,128)S(1)}, f32[16,512]{1,0:T(8,128)}, u32[]{:S(2)}) copy-start(f32[16,512]{1,0:T(8,128)} %param.6) | copy-start | bytes 98308
  12.5 36.5 %collective-permute-start.2 = (bf16[128,2048]{1,0:T(8,128)(2,1)S(1)}, bf16[128,2048]{1,0:T(8,128)(2,1)}, u32[]{:S(2)}, u32[]{:S(2)}) collective-permute-start(bf16[128,2048]{1,0:T(8,128)(2,1)S(1)} %slice.6), channel_id=1, source_target_pairs={{0,8},{4,12},{8,0},{12,4},{1,9},{5,13},{9,1},{13,5},{2,10},{6,14},... | collective-permute-start | bytes 1572872 | tf_op jit(solution)/shard_map/ppermute | solution.py:335
  17.2 29.5 %collective-permute-start = (bf16[192,2048]{1,0:T(8,128)(2,1)S(1)}, bf16[192,2048]{1,0:T(8,128)(2,1)}, u32[]{:S(2)}, u32[]{:S(2)}) collective-permute-start(bf16[192,2048]{1,0:T(8,128)(2,1)S(1)} %get-tuple-element.17), channel_id=1, source_target_pairs={{0,4},{4,8},{8,12},{12,0},{1,5},{5,9},{9,13},{13,1},{2,6},{6,10},{... | collective-permute-start | bytes 2359304 | tf_op jit(solution)/shard_map/ppermute | solution.py:335
  19.4 27.3 %collective-permute-start.1 = (bf16[192,2048]{1,0:T(8,128)(2,1)S(1)}, bf16[192,2048]{1,0:T(8,128)(2,1)}, u32[]{:S(2)}, u32[]{:S(2)}) collective-permute-start(bf16[192,2048]{1,0:T(8,128)(2,1)S(1)} %get-tuple-element.18), channel_id=1, source_target_pairs={{0,12},{4,0},{8,4},{12,8},{1,13},{5,1},{9,5},{13,9},{2,14},{6,2},{... | collective-permute-start | bytes 2359304 | tf_op jit(solution)/shard_map/ppermute | solution.py:335
  23.7 23.0 %copy-start.1 = (bf16[16,512]{1,0:T(8,128)(2,1)}, bf16[16,512]{1,0:T(8,128)(2,1)S(1)}, u32[]{:S(2)}) copy-start(bf16[16,512]{1,0:T(8,128)(2,1)S(1)} %convert_element_type.27) | copy-start | bytes 49156
  24.8 24.2 %all-to-all-start.1 = ((f16[4,4,16,512]{3,2,1,0:T(8,128)(2,1)}), f16[4,4,16,512]{3,2,1,0:T(8,128)(2,1)S(1)}, u32[]{:S(2)}, u32[]{:S(2)}) async-start(f16[4,4,16,512]{3,2,1,0:T(8,128)(2,1)} %broadcast_in_dim.15), calls=%async_computation.1 | async-start | bytes 524288 | tf_op jit(solution)/shard_map/all_to_all | solution.py:167
  59.6 13.5 %all-to-all-start.3 = ((bf16[4,4,4,16,512]{4,3,2,1,0:T(8,128)(2,1)}), bf16[4,4,4,16,512]{4,3,2,1,0:T(8,128)(2,1)S(1)}, u32[]{:S(2)}, u32[]{:S(2)}) async-start(bf16[4,4,4,16,512]{4,3,2,1,0:T(8,128)(2,1)} %broadcast_in_dim.17), calls=%async_computation.3 | async-start | bytes 2097152 | tf_op jit(solution)/shard_map/all_to_all | solution.py:167
  64.6 17.4 %collective-permute-start.3 = (bf16[64,2048]{1,0:T(8,128)(2,1)}, bf16[64,2048]{1,0:T(8,128)(2,1)}, u32[]{:S(2)}, u32[]{:S(2)}) collective-permute-start(bf16[64,2048]{1,0:T(8,128)(2,1)} %slice.7), channel_id=1, source_target_pairs={{0,8},{4,12},{8,0},{12,4},{1,9},{5,13},{9,1},{13,5},{2,10},{6,14},... | collective-permute-start | bytes 786440 | tf_op jit(solution)/shard_map/ppermute | solution.py:335
  73.2 11.9 %collective-permute-start.4 = (bf16[2,2,4,4,16,512]{5,4,3,2,1,0:T(8,128)(2,1)S(1)}, bf16[2,2,4,4,16,512]{5,4,3,2,1,0:T(8,128)(2,1)S(1)}, u32[]{:S(2)}, u32[]{:S(2)}) collective-permute-start(bf16[2,2,4,4,16,512]{5,4,3,2,1,0:T(8,128)(2,1)S(1)} %bitcast.18), channel_id=1, source_target_pairs={{0,1},{1,0},{2,3},{3,2},{4,5},{5,4},{6,7},{7,6},{8,9},{9,8},{10,11... | collective-permute-start | bytes 3145736 | tf_op jit(solution)/shard_map/ppermute | solution.py:349

commit v6 on v4

--- a/solution.py
+++ b/solution.py
@@ -11,146 +11,6 @@
 REPLICAS = 32
 outer_rate = 0.7
 decay_factor = 0.9
-
-
-def exchange(blocks, along, across, turn):
-    n = math.prod(lax.axis_size(a) for a in along)
-    places = list(itertools.product(*(range(lax.axis_size(a)) for a in across)))
-    groups = [[(k + turn(*at)) % n * len(places) + i for k in range(n)] for i, at in enumerate(places)]
-    return lax.all_to_all(blocks, along + across, 0, 0, axis_index_groups=groups, tiled=True)
-
-
-def exchange(blocks, along, across, turn):
-    n = math.prod(lax.axis_size(a) for a in along)
-    places = list(itertools.product(*(range(lax.axis_size(a)) for a in across)))
-    groups = [[(k + turn(*at)) % n * len(places) + i for k in range(n)] for i, at in enumerate(places)]
-    return lax.all_to_all(blocks, along + across, 0, 0, axis_index_groups=groups, tiled=True)
-
-
-def exchange(blocks, along, across, turn):
-    n = math.prod(lax.axis_size(a) for a in along)
-    places = list(itertools.product(*(range(lax.axis_size(a)) for a in across)))
-    groups = [[(k + turn(*at)) % n * len(places) + i for k in range(n)] for i, at in enumerate(places)]
-    return lax.all_to_all(blocks, along + across, 0, 0, axis_index_groups=groups, tiled=True)
-
-
-def exchange(blocks, along, across, turn):
-    n = math.prod(lax.axis_size(a) for a in along)
-    places = list(itertools.product(*(range(lax.axis_size(a)) for a in across)))
-    groups = [[(k + turn(*at)) % n * len(places) + i for k in range(n)] for i, at in enumerate(places)]
-    return lax.all_to_all(blocks, along + across, 0, 0, axis_index_groups=groups, tiled=True)
-
-
-def exchange(blocks, along, across, turn):
-    n = math.prod(lax.axis_size(a) for a in along)
-    places = list(itertools.product(*(range(lax.axis_size(a)) for a in across)))
-    groups = [[(k + turn(*at)) % n * len(places) + i for k in range(n)] for i, at in enumerate(places)]
-    return lax.all_to_all(blocks, along + across, 0, 0, axis_index_groups=groups, tiled=True)
-
-
-def exchange(blocks, along, across, turn):
-    n = math.prod(lax.axis_size(a) for a in along)
-    places = list(itertools.product(*(range(lax.axis_size(a)) for a in across)))
-    groups = [[(k + turn(*at)) % n * len(places) + i for k in range(n)] for i, at in enumerate(places)]
-    return lax.all_to_all(blocks, along + across, 0, 0, axis_index_groups=groups, tiled=True)
-
-
-def exchange(blocks, along, across, turn):
-    n = math.prod(lax.axis_size(a) for a in along)
-    places = list(itertools.product(*(range(lax.axis_size(a)) for a in across)))
-    groups = [[(k + turn(*at)) % n * len(places) + i for k in range(n)] for i, at in enumerate(places)]
-    return lax.all_to_all(blocks, along + across, 0, 0, axis_index_groups=groups, tiled=True)
-
-
-def exchange(blocks, along, across, turn):
-    n = math.prod(lax.axis_size(a) for a in along)
-    places = list(itertools.product(*(range(lax.axis_size(a)) for a in across)))
-    groups = [[(k + turn(*at)) % n * len(places) + i for k in range(n)] for i, at in enumerate(places)]
-    return lax.all_to_all(blocks, along + across, 0, 0, axis_index_groups=groups, tiled=True)
-
-
-def exchange(blocks, along, across, turn):
-    n = math.prod(lax.axis_size(a) for a in along)
-    places = list(itertools.product(*(range(lax.axis_size(a)) for a in across)))
-    groups = [[(k + turn(*at)) % n * len(places) + i for k in range(n)] for i, at in enumerate(places)]
-    return lax.all_to_all(blocks, along + across, 0, 0, axis_index_groups=groups, tiled=True)
-
-
-def exchange(blocks, along, across, turn):
-    n = math.prod(lax.axis_size(a) for a in along)
-    places = list(itertools.product(*(range(lax.axis_size(a)) for a in across)))
-    groups = [[(k + turn(*at)) % n * len(places) + i for k in range(n)] for i, at in enumerate(places)]
-    return lax.all_to_all(blocks, along + across, 0, 0, axis_index_groups=groups, tiled=True)
-
-
-def exchange(blocks, along, across, turn):
-    n = math.prod(lax.axis_size(a) for a in along)
-    places = list(itertools.product(*(range(lax.axis_size(a)) for a in across)))
-    groups = [[(k + turn(*at)) % n * len(places) + i for k in range(n)] for i, at in enumerate(places)]
-    return lax.all_to_all(blocks, along + across, 0, 0, axis_index_groups=groups, tiled=True)
-
-
-def exchange(blocks, along, across, turn):
-    n = math.prod(lax.axis_size(a) for a in along)
-    places = list(itertools.product(*(range(lax.axis_size(a)) for a in across)))
-    groups = [[(k + turn(*at)) % n * len(places) + i for k in range(n)] for i, at in enumerate(places)]
-    return lax.all_to_all(blocks, along + across, 0, 0, axis_index_groups=groups, tiled=True)
-
-
-def exchange(blocks, along, across, turn):
-    n = math.prod(lax.axis_size(a) for a in along)
-    places = list(itertools.product(*(range(lax.axis_size(a)) for a in across)))
-    groups = [[(k + turn(*at)) % n * len(places) + i for k in range(n)] for i, at in enumerate(places)]
-    return lax.all_to_all(blocks, along + across, 0, 0, axis_index_groups=groups, tiled=True)
-
-
-def exchange(blocks, along, across, turn):
-    n = math.prod(lax.axis_size(a) for a in along)
-    places = list(itertools.product(*(range(lax.axis_size(a)) for a in across)))
-    groups = [[(k + turn(*at)) % n * len(places) + i for k in range(n)] for i, at in enumerate(places)]
-    return lax.all_to_all(blocks, along + across, 0, 0, axis_index_groups=groups, tiled=True)
-
-
-def exchange(blocks, along, across, turn):
-    n = math.prod(lax.axis_size(a) for a in along)
-    places = list(itertools.product(*(range(lax.axis_size(a)) for a in across)))
-    groups = [[(k + turn(*at)) % n * len(places) + i for k in range(n)] for i, at in enumerate(places)]
-    return lax.all_to_all(blocks, along + across, 0, 0, axis_index_groups=groups, tiled=True)
-
-
-def exchange(blocks, along, across, turn):
-    n = math.prod(lax.axis_size(a) for a in along)
-    places = list(itertools.product(*(range(lax.axis_size(a)) for a in across)))
-    groups = [[(k + turn(*at)) % n * len(places) + i for k in range(n)] for i, at in enumerate(places)]
-    return lax.all_to_all(blocks, along + across, 0, 0, axis_index_groups=groups, tiled=True)
-
-
-def exchange(blocks, along, across, turn):
-    n = math.prod(lax.axis_size(a) for a in along)
-    places = list(itertools.product(*(range(lax.axis_size(a)) for a in across)))
-    groups = [[(k + turn(*at)) % n * len(places) + i for k in range(n)] for i, at in enumerate(places)]
-    return lax.all_to_all(blocks, along + across, 0, 0, axis_index_groups=groups, tiled=True)
-
-
-def exchange(blocks, along, across, turn):
-    n = math.prod(lax.axis_size(a) for a in along)
-    places = list(itertools.product(*(range(lax.axis_size(a)) for a in across)))
-    groups = [[(k + turn(*at)) % n * len(places) + i for k in range(n)] for i, at in enumerate(places)]
-    return lax.all_to_all(blocks, along + across, 0, 0, axis_index_groups=groups, tiled=True)
-
-
-def exchange(blocks, along, across, turn):
-    n = math.prod(lax.axis_size(a) for a in along)
-    places = list(itertools.product(*(range(lax.axis_size(a)) for a in across)))
-    groups = [[(k + turn(*at)) % n * len(places) + i for k in range(n)] for i, at in enumerate(places)]
-    return lax.all_to_all(blocks, along + across, 0, 0, axis_index_groups=groups, tiled=True)
-
-
-def exchange(blocks, along, across, turn):
-    n = math.prod(lax.axis_size(a) for a in along)
-    places = list(itertools.product(*(range(lax.axis_size(a)) for a in across)))
-    groups = [[(k + turn(*at)) % n * len(places) + i for k in range(n)] for i, at in enumerate(places)]
-    return lax.all_to_all(blocks, along + across, 0, 0, axis_index_groups=groups, tiled=True)
 
 
 def exchange(blocks, along, across, turn):
@@ -320,7 +180,7 @@
     sums = jnp.sum(sums.astype(jnp.float32), axis=0)
     fresh = (gain * sums).astype(jnp.bfloat16)
 
-    most = tok // 2
+    most = tok * 2 // 3
     cuts = [lax.dynamic_slice(tokens, (0, (x + d) % nx * part), (tok, part)) for d in (1, 3, 2)]
     cuts = lax.optimization_barrier(cuts)
     cuts[2:] = lax.optimization_barrier([cuts[2][:most], cuts[2][most:]])

time: 102 us -> 101 us (level)
  blocking collectives: 26.1 us -> 22.1 us
  starting transfers between devices: 48.5 us -> 50.6 us
  waiting for transfers between devices: 9.62 us -> 10.8 us
    all_to_all x2, blocking collectives: 26.1 us -> 22.1 us  [exchange(): lax.all_to_all(blocks, along + across, 0, 0, axis_index_groups=groups, ti...]
    ppermute x4, waiting for transfers between devices: 4.41 us -> 7.75 us  [local(): lax.ppermute(cut, 'x', [(i, (i + d) % nx) for i in range(nx)])]
    ppermute x4, starting transfers between devices: 13 us -> 15.2 us  [local(): lax.ppermute(cut, 'x', [(i, (i + d) % nx) for i in range(nx)])]
    all_to_all x2, waiting for transfers between devices: 5.2 us -> 3.08 us  [exchange(): lax.all_to_all(blocks, along + across, 0, 0, axis_index_groups=groups, ti...]
where the time goes in v6:
time: 101 us; the launch traced here: 100 us
  starting transfers between devices  50.6 us (50%)
  blocking collectives  22.1 us (22%)
  waiting for transfers between devices  10.8 us (11%)
  Pallas kernels  6.75 us (7%)
  local copies, waits for them, and re-layouts  6.28 us (6%)
  other arithmetic  2.62 us (3%)
    all_to_all x2, blocking collectives, exchange(): lax.all_to_all(blocks, along + across, 0, 0, axis_index_groups=groups, ti...  22.1 us
    all_to_all x2, starting transfers between devices, exchange(): lax.all_to_all(blocks, along + across, 0, 0, axis_index_groups=groups, ti...  19.2 us
    ppermute x4, starting transfers between devices, local(): lax.ppermute(cut, 'x', [(i, (i + d) % nx) for i in range(nx)])  15.2 us
    ppermute x1, starting transfers between devices, local(): other = lax.ppermute(rows_y, 'c', [(0, 1), (1, 0)])  8.8 us
    ppermute x4, waiting for transfers between devices, local(): lax.ppermute(cut, 'x', [(i, (i + d) % nx) for i in range(nx)])  7.75 us
    all_to_all x1, starting transfers between devices, local(): near = lax.all_to_all(trained, ('zl', 'yl'), 1, 1, tiled=True)  7.46 us
    all_to_all x2, waiting for transfers between devices, exchange(): lax.all_to_all(blocks, along + across, 0, 0, axis_index_groups=groups, ti...  3.08 us
    pallas_call x1, Pallas kernels, gather_tokens(): pl.pallas_call(gather_kernel, in_specs=specs, **moved((3,) + t1.shape, 3))  2.18 us
  transfers between devices with their start and end apart: 8, of which 2 were waited for; matrix products, arithmetic and copies ran while one was open for 5% of the time, Pallas kernels for 5%

profile of v6, /device:TPU:1, one launch (start us, length us, event | category | flops | bytes accessed | tf_op | source)
XLA Modules:
  0.0 100.1 jit_solution(4499476127922497834)
XLA Ops:
  0.6 1.9 %copy.9 = bf16[4,8,16,512]{3,2,0,1:T(8,128)(2,1)} copy(bf16[4,8,16,512]{3,2,1,0:T(8,128)(2,1)} %bitcast.20) | data formatting | bytes 1048576 | tf_op jit(solution)/shard_map/reshape;squeeze | solution.py:169
  2.5 7.5 %all-to-all-start = ((bf16[4,8,16,512]{3,2,0,1:T(8,128)(2,1)}), bf16[4,8,16,512]{3,2,0,1:T(8,128)(2,1)S(1)}, u32[]{:S(2)}, u32[]{:S(2)}) async-start(bf16[4,8,16,512]{3,2,0,1:T(8,128)(2,1)} %copy.9), calls=%async_computation | async-start | bytes 1048576 | tf_op jit(solution)/shard_map/all_to_all | solution.py:170
  10.0 0.0 copy-start
  10.0 0.0 copy-start.2
  10.0 1.8 %constant_dynamic-slice_fusion = (bf16[192,2048]{1,0:T(8,128)(2,1)S(1)}, bf16[192,2048]{1,0:T(8,128)(2,1)S(1)}, bf16[192,2048]{1,0:T(8,128)(2,1)S(1)}) fusion(bf16[192,8192]{1,0:T(8,128)(2,1)} %tokens.1, s32[]{:T(128)S(6)} %select_n.42, s32[]{:T(128)S(6)} %select_n.40, s32[]{:T(128)S(6)} %select_n.38), kind=kLoop, calls=%fused_computation.16 | loop fusion | bytes 4718604 | tf_op jit(solution)/shard_map/dynamic_slice | solution.py:184
  11.8 0.7 slice.7
  12.5 4.7 %collective-permute-start.2 = (bf16[128,2048]{1,0:T(8,128)(2,1)S(1)}, bf16[128,2048]{1,0:T(8,128)(2,1)}, u32[]{:S(2)}, u32[]{:S(2)}) collective-permute-start(bf16[128,2048]{1,0:T(8,128)(2,1)S(1)} %slice.6), channel_id=1, source_target_pairs={{0,8},{4,12},{8,0},{12,4},{1,9},{5,13},{9,1},{13,5},{2,10},{6,14},... | collective-permute-start | bytes 1572872 | tf_op jit(solution)/shard_map/ppermute | solution.py:188
  17.2 2.2 %collective-permute-start = (bf16[192,2048]{1,0:T(8,128)(2,1)S(1)}, bf16[192,2048]{1,0:T(8,128)(2,1)}, u32[]{:S(2)}, u32[]{:S(2)}) collective-permute-start(bf16[192,2048]{1,0:T(8,128)(2,1)S(1)} %get-tuple-element.17), channel_id=1, source_target_pairs={{0,4},{4,8},{8,12},{12,0},{1,5},{5,9},{9,13},{13,1},{2,6},{6,10},{... | collective-permute-start | bytes 2359304 | tf_op jit(solution)/shard_map/ppermute | solution.py:188
  19.4 4.3 %collective-permute-start.1 = (bf16[192,2048]{1,0:T(8,128)(2,1)S(1)}, bf16[192,2048]{1,0:T(8,128)(2,1)}, u32[]{:S(2)}, u32[]{:S(2)}) collective-permute-start(bf16[192,2048]{1,0:T(8,128)(2,1)S(1)} %get-tuple-element.18), channel_id=1, source_target_pairs={{0,12},{4,0},{8,4},{12,8},{1,13},{5,1},{9,5},{13,9},{2,14},{6,2},{... | collective-permute-start | bytes 2359304 | tf_op jit(solution)/shard_map/ppermute | solution.py:188
  23.7 0.0 copy-done
  23.7 0.0 copy-start.1
  23.8 0.1 pad_add_fusion.at
  23.8 0.0 copy-done.2
  23.9 0.0 all-to-all-done
  23.9 0.1 convert_reduce_fusion.1
  24.0 0.1 fusion
  24.0 0.7 broadcast_in_dim.15
  24.8 14.2 %all-to-all-start.1 = ((f16[4,4,16,512]{3,2,1,0:T(8,128)(2,1)}), f16[4,4,16,512]{3,2,1,0:T(8,128)(2,1)S(1)}, u32[]{:S(2)}, u32[]{:S(2)}) async-start(f16[4,4,16,512]{3,2,1,0:T(8,128)(2,1)} %broadcast_in_dim.15), calls=%async_computation.1 | async-start | bytes 524288 | tf_op jit(solution)/shard_map/all_to_all | solution.py:20
  39.0 7.7 %collective-permute-done.t1 = bf16[192,2048]{1,0:T(8,128)(2,1)} collective-permute-done((bf16[192,2048]{1,0:T(8,128)(2,1)S(1)}, bf16[192,2048]{1,0:T(8,128)(2,1)}, u32[]{:S(2)}, u32[]{:S(2)}) %collective-permute-start) | collective-permute-done | bytes 786464 | tf_op jit(solution)/shard_map/ppermute | solution.py:188
  46.7 0.0 copy-done.1
  46.7 0.0 collective-permute-done.1.t3
  46.7 2.2 %shard_map.75.near = bf16[3,192,2048]{2,1,0:T(8,128)(2,1)S(1)} custom-call(s32[4]{0:T(128)S(1)} %pad_add_fusion.at, bf16[192,8192]{1,0:T(8,128)(2,1)} %tokens.1, bf16[192,2048]{1,0:T(8,128)(2,1)} %collective-permute-done.t1, bf16[192,2048]{1,0:T(8,128)(2,1)} %collective-permute-done.1.t3), custom_call_target="tpu_custom_call" | custom-call | flops 17179869184 | bytes 67108864 | tf_op jit(solution)/shard_map/pallas_call | solution.py:75
  48.9 0.0 all-to-all-done.1
  49.0 0.0 collective-permute-done.2.first
  49.0 9.5 %all_to_all.25 = bf16[4,4,16,512]{3,2,1,0:T(8,128)(2,1)S(1)} all-to-all(bf16[4,4,16,512]{3,2,1,0:T(8,128)(2,1)S(1)} %broadcast_in_dim.16), channel_id=1, replica_groups={{0,32,64,96},{65,97,1,33},{2,34,66,98},{67,99,3,35},{4,36,68,100},{69,1..., dimensions={0} | all-to-all | bytes 524288 | tf_op jit(solution)/shard_map/all_to_all | solution.py:20
  58.5 1.1 %broadcast_in_dim.17 = bf16[4,4,4,16,512]{4,3,2,1,0:T(8,128)(2,1)} broadcast(bf16[4,4,16,512]{3,2,1,0:T(8,128)(2,1)S(1)} %all_to_all.25), dimensions={1,2,3,4} | broadcast | bytes 1310720 | tf_op jit(solution)/shard_map/broadcast_in_dim | solution.py:25
  59.6 5.0 %all-to-all-start.3 = ((bf16[4,4,4,16,512]{4,3,2,1,0:T(8,128)(2,1)}), bf16[4,4,4,16,512]{4,3,2,1,0:T(8,128)(2,1)S(1)}, u32[]{:S(2)}, u32[]{:S(2)}) async-start(bf16[4,4,4,16,512]{4,3,2,1,0:T(8,128)(2,1)} %broadcast_in_dim.17), calls=%async_computation.3 | async-start | bytes 2097152 | tf_op jit(solution)/shard_map/all_to_all | solution.py:20
  64.6 4.0 %collective-permute-start.3 = (bf16[64,2048]{1,0:T(8,128)(2,1)}, bf16[64,2048]{1,0:T(8,128)(2,1)}, u32[]{:S(2)}, u32[]{:S(2)}) collective-permute-start(bf16[64,2048]{1,0:T(8,128)(2,1)} %slice.7), channel_id=1, source_target_pairs={{0,8},{4,12},{8,0},{12,4},{1,9},{5,13},{9,1},{13,5},{2,10},{6,14},... | collective-permute-start | bytes 786440 | tf_op jit(solution)/shard_map/ppermute | solution.py:188
  68.6 1.4 %multiply_add_fusion = (f32[16,512]{1,0:T(8,128)}, f32[16,512]{1,0:T(8,128)}) fusion(f32[16,512]{1,0:T(8,128)} %param.6, f32[4,16,512]{2,1,0:T(8,128)S(1)} %convert_reduce_fusion.2, s32[]{:T(128)S(6)} %select_n.43, bf16[16,512]{1,0:T(8,128)(2,1)} %copy-done.1, f32[16,512]{1,0:T(8,128)} %param.5), kind=kLoop, calls=%fused_computation.15 | loop fusion | flops 131072 | bytes 180228 | tf_op jit(solution)/shard_map/add | solution.py:198
  70.1 3.1 %all-to-all-done.3 = bf16[4,4,4,16,512]{4,3,2,1,0:T(8,128)(2,1)S(1)} async-done(((bf16[4,4,4,16,512]{4,3,2,1,0:T(8,128)(2,1)}), bf16[4,4,4,16,512]{4,3,2,1,0:T(8,128)(2,1)S(1)}, u32[]{:S(2)}, u32[]{:S(2)}) %all-to-all-start.3) | async-done | bytes 1048608 | tf_op jit(solution)/shard_map/all_to_all | solution.py:20
  73.2 8.8 %collective-permute-start.4 = (bf16[2,2,4,4,16,512]{5,4,3,2,1,0:T(8,128)(2,1)S(1)}, bf16[2,2,4,4,16,512]{5,4,3,2,1,0:T(8,128)(2,1)S(1)}, u32[]{:S(2)}, u32[]{:S(2)}) collective-permute-start(bf16[2,2,4,4,16,512]{5,4,3,2,1,0:T(8,128)(2,1)S(1)} %bitcast.18), channel_id=1, source_target_pairs={{0,1},{1,0},{2,3},{3,2},{4,5},{5,4},{6,7},{7,6},{8,9},{9,8},{10,11... | collective-permute-start | bytes 3145736 | tf_op jit(solution)/shard_map/ppermute | solution.py:202
  82.0 0.0 collective-permute-done.3.second
  82.0 1.1 %shard_map.76.far = bf16[192,2048]{1,0:T(8,128)(2,1)S(1)} custom-call(bf16[128,2048]{1,0:T(8,128)(2,1)} %collective-permute-done.2.first, bf16[64,2048]{1,0:T(8,128)(2,1)} %collective-permute-done.3.second), custom_call_target="tpu_custom_call" | custom-call | flops 17179869184 | bytes 67108864 | tf_op jit(solution)/shard_map/pallas_call | solution.py:80
  83.1 1.9 %shard_map.77 = (f32[768,512]{1,0:T(8,128)S(1)}, bf16[512,512]{1,0:T(8,128)(2,1)}) custom-call(s32[4]{0:T(128)S(1)} %pad_add_fusion.at, bf16[2,2,4,4,16,512]{5,4,3,2,1,0:T(8,128)(2,1)S(1)} %bitcast.19, bf16[3,192,2048]{2,1,0:T(8,128)(2,1)S(1)} %shard_map.75.near, bf16[192,2048]{1,0:T(8,128)(2,1)S(1)} %shard_map.76.far), custom_call_target="tpu_custom_call" | custom-call | flops 805306368 | bytes 4194304 | tf_op jit(solution)/shard_map/pallas_call | solution.py:135
  85.0 0.0 collective-permute-done.4.rows_y
  85.0 1.5 %shard_map.78 = bf16[4,192,512]{2,1,0:T(8,128)(2,1)S(1)} custom-call(s32[4]{0:T(128)S(1)} %pad_add_fusion.at, bf16[2,2,4,4,16,512]{5,4,3,2,1,0:T(8,128)(2,1)S(1)} %collective-permute-done.4.rows_y, bf16[3,192,2048]{2,1,0:T(8,128)(2,1)S(1)} %shard_map.75.near, bf16[192,2048]{1,0:T(8,128)(2,1)S(1)} %shard_map.76.far, f32[768,512]{1,0:T(8,128)S(1)} %get-tuple-element.29.total), custom_call_target="tpu_custom_call" | custom-call | flops 805306368 | bytes 4194304 | tf_op jit(solution)/shard_map/pallas_call | solution.py:151
  86.6 12.6 %all_to_all.26 = bf16[4,192,512]{2,1,0:T(8,128)(2,1)S(1)} all-to-all(bf16[4,192,512]{2,1,0:T(8,128)(2,1)S(1)} %shard_map.78), channel_id=1, replica_groups={{0,4,8,12},{9,13,1,5},{2,6,10,14},{11,15,3,7},{16,20,24,28},{25,29,17,2..., dimensions={0} | all-to-all | bytes 1572864 | tf_op jit(solution)/shard_map/all_to_all | solution.py:20
  99.2 0.9 convert_reduce_fusion
  (7 shorter events, 0.1 us)
Async XLA Ops:
  2.5 21.4 %all-to-all-start = ((bf16[4,8,16,512]{3,2,0,1:T(8,128)(2,1)}), bf16[4,8,16,512]{3,2,0,1:T(8,128)(2,1)S(1)}, u32[]{:S(2)}, u32[]{:S(2)}) async-start(bf16[4,8,16,512]{3,2,0,1:T(8,128)(2,1)} %copy.9), calls=%async_computation | async-start | bytes 1048576 | tf_op jit(solution)/shard_map/all_to_all | solution.py:170
  10.0 13.7 %copy-start = (f32[16,512]{1,0:T(8,128)S(1)}, f32[16,512]{1,0:T(8,128)}, u32[]{:S(2)}) copy-start(f32[16,512]{1,0:T(8,128)} %param.5) | copy-start | bytes 98308
  10.0 13.9 %copy-start.2 = (f32[16,512]{1,0:T(8,128)S(1)}, f32[16,512]{1,0:T(8,128)}, u32[]{:S(2)}) copy-start(f32[16,512]{1,0:T(8,128)} %param.6) | copy-start | bytes 98308
  12.5 36.5 %collective-permute-start.2 = (bf16[128,2048]{1,0:T(8,128)(2,1)S(1)}, bf16[128,2048]{1,0:T(8,128)(2,1)}, u32[]{:S(2)}, u32[]{:S(2)}) collective-permute-start(bf16[128,2048]{1,0:T(8,128)(2,1)S(1)} %slice.6), channel_id=1, source_target_pairs={{0,8},{4,12},{8,0},{12,4},{1,9},{5,13},{9,1},{13,5},{2,10},{6,14},... | collective-permute-start | bytes 1572872 | tf_op jit(solution)/shard_map/ppermute | solution.py:188
  17.2 29.5 %collective-permute-start = (bf16[192,2048]{1,0:T(8,128)(2,1)S(1)}, bf16[192,2048]{1,0:T(8,128)(2,1)}, u32[]{:S(2)}, u32[]{:S(2)}) collective-permute-start(bf16[192,2048]{1,0:T(8,128)(2,1)S(1)} %get-tuple-element.17), channel_id=1, source_target_pairs={{0,4},{4,8},{8,12},{12,0},{1,5},{5,9},{9,13},{13,1},{2,6},{6,10},{... | collective-permute-start | bytes 2359304 | tf_op jit(solution)/shard_map/ppermute | solution.py:188
  19.4 27.3 %collective-permute-start.1 = (bf16[192,2048]{1,0:T(8,128)(2,1)S(1)}, bf16[192,2048]{1,0:T(8,128)(2,1)}, u32[]{:S(2)}, u32[]{:S(2)}) collective-permute-start(bf16[192,2048]{1,0:T(8,128)(2,1)S(1)} %get-tuple-element.18), channel_id=1, source_target_pairs={{0,12},{4,0},{8,4},{12,8},{1,13},{5,1},{9,5},{13,9},{2,14},{6,2},{... | collective-permute-start | bytes 2359304 | tf_op jit(solution)/shard_map/ppermute | solution.py:188
  23.7 23.0 %copy-start.1 = (bf16[16,512]{1,0:T(8,128)(2,1)}, bf16[16,512]{1,0:T(8,128)(2,1)S(1)}, u32[]{:S(2)}) copy-start(bf16[16,512]{1,0:T(8,128)(2,1)S(1)} %convert_element_type.27) | copy-start | bytes 49156
  24.8 24.2 %all-to-all-start.1 = ((f16[4,4,16,512]{3,2,1,0:T(8,128)(2,1)}), f16[4,4,16,512]{3,2,1,0:T(8,128)(2,1)S(1)}, u32[]{:S(2)}, u32[]{:S(2)}) async-start(f16[4,4,16,512]{3,2,1,0:T(8,128)(2,1)} %broadcast_in_dim.15), calls=%async_computation.1 | async-start | bytes 524288 | tf_op jit(solution)/shard_map/all_to_all | solution.py:20
  59.6 13.5 %all-to-all-start.3 = ((bf16[4,4,4,16,512]{4,3,2,1,0:T(8,128)(2,1)}), bf16[4,4,4,16,512]{4,3,2,1,0:T(8,128)(2,1)S(1)}, u32[]{:S(2)}, u32[]{:S(2)}) async-start(bf16[4,4,4,16,512]{4,3,2,1,0:T(8,128)(2,1)} %broadcast_in_dim.17), calls=%async_computation.3 | async-start | bytes 2097152 | tf_op jit(solution)/shard_map/all_to_all | solution.py:20
  64.6 17.4 %collective-permute-start.3 = (bf16[64,2048]{1,0:T(8,128)(2,1)}, bf16[64,2048]{1,0:T(8,128)(2,1)}, u32[]{:S(2)}, u32[]{:S(2)}) collective-permute-start(bf16[64,2048]{1,0:T(8,128)(2,1)} %slice.7), channel_id=1, source_target_pairs={{0,8},{4,12},{8,0},{12,4},{1,9},{5,13},{9,1},{13,5},{2,10},{6,14},... | collective-permute-start | bytes 786440 | tf_op jit(solution)/shard_map/ppermute | solution.py:188
  73.2 11.9 %collective-permute-start.4 = (bf16[2,2,4,4,16,512]{5,4,3,2,1,0:T(8,128)(2,1)S(1)}, bf16[2,2,4,4,16,512]{5,4,3,2,1,0:T(8,128)(2,1)S(1)}, u32[]{:S(2)}, u32[]{:S(2)}) collective-permute-start(bf16[2,2,4,4,16,512]{5,4,3,2,1,0:T(8,128)(2,1)S(1)} %bitcast.18), channel_id=1, source_target_pairs={{0,1},{1,0},{2,3},{3,2},{4,5},{5,4},{6,7},{7,6},{8,9},{9,8},{10,11... | collective-permute-start | bytes 3145736 | tf_op jit(solution)/shard_map/ppermute | solution.py:202
